TPU v7x, 32 devices: a whole 2x2x4 slice. The times are simulated.
32 devices in a mesh: seq: 8 (over z, y), chan: 4 (over x, core).
Axes of the slice: x: 2, y: 2, z: 4, core: 2. Of those that a mesh axis runs over, the one named last changes fastest.
Arguments:
- inputs: bfloat16 [2, 1024, 1024], P(None, 'seq', 'chan'), may hold values from -6 to 6
- lengths: int32 [2], replicated, may hold values from 256 to 1024, as said below
- out_grad: bfloat16 [2, 1024, 1024], P(None, 'seq', 'chan'), may hold values from -6 to 6
- norm_gain: bfloat16 [1024], P('chan'), may hold values from 0.5 to 1.5
- input_projection_weight: bfloat16 [2, 1024, 2048], P(None, None, 'chan'), may hold values from -0.1875 to 0.1875
- conv_weight: float32 [4, 2048], P(None, 'chan'), may hold values from -3 to 3
- conv_bias: float32 [2048], P('chan'), may hold values from -1 to 1
- x_weight: bfloat16 [96, 2048], P(None, 'chan'), may hold values from -0.125 to 0.125
- dt_weight: bfloat16 [64, 2048], P(None, 'chan'), may hold values from -0.75 to 0.75
- dt_bias: float32 [2048], P('chan'), may hold values from -7 to -2
- log_decay: float32 [16, 2048], P(None, 'chan'), may hold values from -5 to 1
- skip_gain: float32 [2048], P('chan'), may hold values from 0.5 to 1.5
- output_projection_weight: bfloat16 [2048, 1024], P('chan'), may hold values from -0.5 to 0.5
Outputs:
- mixed_out: bfloat16 [2, 1024, 1024], P(None, 'seq', 'chan')
- grad_inputs: bfloat16 [2, 1024, 1024], P(None, 'seq', 'chan')
- grad_norm_gain: float32 [1024], P('chan')
- grad_in_weight: float32 [2, 1024, 2048], P(None, None, 'chan')
- grad_conv_weight: float32 [4, 2048], P(None, 'chan')
- grad_conv_bias: float32 [2048], P('chan')
- grad_x_weight: float32 [96, 2048], P(None, 'chan')
- grad_dt_weight: float32 [64, 2048], P(None, 'chan')
- grad_dt_bias: float32 [2048], P('chan')
- grad_log_decay: float32 [16, 2048], P(None, 'chan')
- grad_skip_gain: float32 [2048], P('chan')
- grad_out_weight: float32 [2048, 1024], P('chan')
Inputs may be any that keep to these rules, and one draw needn't show every extreme that they name: `lengths`: each sequence's valid tokens come first and padding fills the rest; one sequence fills all 1024 positions.
All inputs are finite; a program needn't handle non-finite values.
Results may differ from a plain program's by a relative error of at most 0.0086.
Values may be sent and summed in bfloat16 or wider, within the bound.
A program may use at most 128 MiB of HBM per device.

v0:
```python
from functools import partial
import jax
import jax.numpy as jnp
from jax import lax
from jax.experimental import pallas as pl
from jax.experimental.pallas import tpu as pltpu
from jax.sharding import PartitionSpec as P

epsilon = 1e-05


def from_behind(value, axis, steps):
    count = lax.axis_size(axis)
    first, last = (max(0, -steps), min(count, count - steps))
    return lax.ppermute(value, axis, [(source, source + steps) for source in range(first, last)])


def carried_in(totals, rate2, ends, leaves):
    count, mine = (lax.axis_size("seq"), lax.axis_index("seq"))
    all_totals, all_ends, all_leaves = (
        lax.all_gather(part, "seq") for part in (totals, ends, leaves)
    )
    entering, leaving = (jnp.zeros_like(ends), jnp.zeros_like(leaves))

    def turn(step, pair):
        entering, leaving = pair
        earlier, later = (step, count - 1 - step)
        forward = jnp.exp2(all_totals[earlier][:, None, :] * rate2) * entering + all_ends[earlier]
        backward = jnp.exp2(all_totals[later][:, None, :] * rate2) * leaving + all_leaves[later]
        return (
            jnp.where(earlier < mine, forward, entering),
            jnp.where(later > mine, backward, leaving),
        )

    return lax.fori_loop(0, count - 1, turn, (entering, leaving))


def silu_slope(values):
    sigmoid_val = jax.nn.sigmoid(values)
    return sigmoid_val * (1.0 + values * (1.0 - sigmoid_val))


LANES = 128
LOG2E = 1.4426950408889634


def lane_chunks(width):
    return [slice(k * LANES, (k + 1) * LANES) for k in range(width // LANES)]


def spread_maps(maps_ref, b_ref, c_ref, states, first, tokens):
    def block(index, _):
        start = index * 8
        rolled = pltpu.roll(maps_ref[:, first : first + tokens], lax.rem(tokens - start, tokens), 1)
        for j in range(8):
            column = jnp.broadcast_to(rolled[:, j : j + 1], (2 * states, LANES))
            b_ref[first + start + j] = column[:states]
            c_ref[first + start + j] = column[states:]
        return 0

    lax.fori_loop(0, tokens // 8, block, 0)


def local_states(decay_ref, step_ref, drive_ref, b_ref, rate_ref, first, tokens):
    states, width = rate_ref.shape
    chunks = lane_chunks(width)

    def block(index, held):
        held = list(held)
        rows = pl.ds(pl.multiple_of(first + index * 8, 8), 8)
        steps = [step_ref[rows, lanes] for lanes in chunks]
        drives = [drive_ref[rows, lanes] for lanes in chunks]
        for j in range(8):
            token = first + index * 8 + j
            b = b_ref[token]
            for k, lanes in enumerate(chunks):
                decay = jnp.exp2(steps[k][j : j + 1] * rate_ref[:, lanes])
                decay_ref[token, :, lanes] = decay
                held[k] = decay * held[k] + drives[k][j : j + 1] * b
        return tuple(held)

    zero = tuple(jnp.zeros((states, LANES), jnp.float32) for _ in chunks)
    return lax.fori_loop(0, tokens // 8, block, zero)


def local_adjoints(decay_ref, up_ref, c_ref, first, tokens):
    _, states, width = decay_ref.shape
    chunks = lane_chunks(width)

    def block(index, held):
        held = list(held)
        start = first + (tokens // 8 - 1 - index) * 8
        ups = [up_ref[pl.ds(pl.multiple_of(start, 8), 8), lanes] for lanes in chunks]
        for j in range(7, -1, -1):
            token = start + j
            c = c_ref[token]
            for k, lanes in enumerate(chunks):
                adjoint = c * ups[k][j : j + 1] + held[k]
                held[k] = decay_ref[token, :, lanes] * adjoint
        return tuple(held)

    zero = tuple(jnp.zeros((states, LANES), jnp.float32) for _ in chunks)
    return lax.fori_loop(0, tokens // 8, block, zero)


def run_states(decay_ref, drive_ref, b_ref, c_ref, enter_ref, state_ref, out_ref, which, first, tokens):
    _, states, width = decay_ref.shape
    chunks = lane_chunks(width)

    def block(index, held):
        held = list(held)
        rows = pl.ds(pl.multiple_of(first + index * 8, 8), 8)
        drives = [drive_ref[rows, lanes] for lanes in chunks]
        outs = [[] for _ in chunks]
        for j in range(8):
            token = first + index * 8 + j
            b, c = b_ref[token], c_ref[token]
            for k, lanes in enumerate(chunks):
                held[k] = decay_ref[token, :, lanes] * held[k] + drives[k][j : j + 1] * b
                state_ref[token, :, lanes] = held[k].astype(jnp.bfloat16)
                outs[k].append(jnp.sum(c * held[k], axis=0, keepdims=True))
        for k, lanes in enumerate(chunks):
            out_ref[rows, lanes] = jnp.concatenate(outs[k], axis=0)
        return tuple(held)

    start = tuple(enter_ref[which, :, lanes] for lanes in chunks)
    lax.fori_loop(0, tokens // 8, block, start)


def run_adjoints(
    decay_ref, step_ref, up_ref, b_ref, c_ref, rate_ref, enter_ref, leave_ref, state_ref,
    adjoint_ref, first_sum_ref, second_sum_ref, which, first, tokens,
):
    _, states, width = decay_ref.shape
    chunks = lane_chunks(width)

    def block(index, carried):
        held, total = list(carried[0]), list(carried[1])
        ones = [[None] * 8 for _ in chunks]
        twos = [[None] * 8 for _ in chunks]
        start = first + (tokens // 8 - 1 - index) * 8
        rows = pl.ds(pl.multiple_of(start, 8), 8)
        ups = [up_ref[rows, lanes] for lanes in chunks]
        steps = [step_ref[rows, lanes] for lanes in chunks]
        for j in range(7, -1, -1):
            token = start + j
            b, c = b_ref[token], c_ref[token]
            for k, lanes in enumerate(chunks):
                adjoint = c * ups[k][j : j + 1] + held[k]
                adjoint_ref[token, :, lanes] = adjoint.astype(jnp.bfloat16)
                held[k] = decay_ref[token, :, lanes] * adjoint
                if j > 0:
                    before = state_ref[token - 1, :, lanes].astype(jnp.float32)
                else:
                    before = state_ref[jnp.maximum(token - 1, first), :, lanes].astype(jnp.float32)
                    before = jnp.where(token == first, enter_ref[which, :, lanes], before)
                pulled = held[k] * before
                ones[k][j] = jnp.sum(pulled * rate_ref[:, lanes], axis=0, keepdims=True)
                twos[k][j] = jnp.sum(adjoint * b, axis=0, keepdims=True)
                total[k] = total[k] + pulled * steps[k][j : j + 1]
        for k, lanes in enumerate(chunks):
            first_sum_ref[rows, lanes] = jnp.concatenate(ones[k], axis=0)
            second_sum_ref[rows, lanes] = jnp.concatenate(twos[k], axis=0)
        return tuple(held), tuple(total)

    begin = tuple(leave_ref[which, :, lanes] for lanes in chunks)
    zero = tuple(jnp.zeros((states, LANES), jnp.float32) for _ in chunks)
    return lax.fori_loop(0, tokens // 8, block, (begin, zero))[1]


def map_sums(values_ref, rows, states, first, tokens):
    width = rows.shape[1]
    flat = values_ref[first : first + tokens].reshape(tokens * states, width)
    all_pairs = lax.dot_general(
        flat, rows.astype(jnp.bfloat16), (((1,), (1,)), ((), ())), preferred_element_type=jnp.float32
    )
    row_token = lax.broadcasted_iota(jnp.int32, (tokens * states, tokens), 0) // states
    column_token = lax.broadcasted_iota(jnp.int32, (tokens * states, tokens), 1)
    kept = jnp.where(row_token == column_token, all_pairs, 0.0).astype(jnp.bfloat16)
    state = lax.broadcasted_iota(jnp.int32, (states, tokens * states), 0)
    row_state = lax.broadcasted_iota(jnp.int32, (states, tokens * states), 1) % states
    pick = (state == row_state).astype(jnp.bfloat16)
    return jnp.dot(pick, kept, preferred_element_type=jnp.float32)


def summary_kernel(seqs, step_ref, drive_ref, up_ref, maps_ref, rate_ref, end_ref, leave_ref, decay_ref, b_ref, c_ref):
    states, width = rate_ref.shape
    tokens = step_ref.shape[0] // seqs
    for s in range(seqs):
        spread_maps(maps_ref, b_ref, c_ref, states, s * tokens, tokens)
        ends = local_states(decay_ref, step_ref, drive_ref, b_ref, rate_ref, s * tokens, tokens)
        for k, lanes in enumerate(lane_chunks(width)):
            end_ref[s, :, lanes] = ends[k]
        leaves = local_adjoints(decay_ref, up_ref, c_ref, s * tokens, tokens)
        for k, lanes in enumerate(lane_chunks(width)):
            leave_ref[s, :, lanes] = leaves[k]


def scan_kernel(
    seqs, step_ref, drive_ref, up_ref, maps_ref, rate2_ref, rate_ref, enter_ref, leave_ref,
    out_ref, first_sum_ref, second_sum_ref, maps_grad_ref, rate_sum_ref,
    decay_ref, b_ref, c_ref, state_ref, adjoint_ref,
):
    states, width = rate_ref.shape
    tokens = step_ref.shape[0] // seqs
    for s in range(seqs):
        first = s * tokens
        spread_maps(maps_ref, b_ref, c_ref, states, first, tokens)
        local_states(decay_ref, step_ref, drive_ref, b_ref, rate2_ref, first, tokens)
        run_states(decay_ref, drive_ref, b_ref, c_ref, enter_ref, state_ref, out_ref, s, first, tokens)
        sums = run_adjoints(
            decay_ref, step_ref, up_ref, b_ref, c_ref, rate_ref, enter_ref, leave_ref, state_ref,
            adjoint_ref, first_sum_ref, second_sum_ref, s, first, tokens,
        )
        for k, lanes in enumerate(lane_chunks(width)):
            if s == 0:
                rate_sum_ref[:, lanes] = sums[k]
            else:
                rate_sum_ref[:, lanes] += sums[k]
        maps_grad_ref[:states, first : first + tokens] = map_sums(
            adjoint_ref, drive_ref[first : first + tokens], states, first, tokens
        )
        maps_grad_ref[states:, first : first + tokens] = map_sums(
            state_ref, up_ref[first : first + tokens], states, first, tokens
        )


VMEM_LIMIT = 60 * 2**20


def whole(count):
    return [pl.BlockSpec(memory_space=pltpu.VMEM)] * count


def scan_summary(step, drive, up, maps, rate2, seqs):
    states, width = rate2.shape
    rows = step.shape[0]
    small = jax.ShapeDtypeStruct((seqs, states, width), jnp.float32)
    return pl.pallas_call(
        partial(summary_kernel, seqs),
        out_shape=(small, small),
        in_specs=whole(5),
        out_specs=tuple(whole(2)),
        scratch_shapes=[
            pltpu.VMEM((rows, states, width), jnp.float32),
            pltpu.VMEM((rows, states, LANES), jnp.float32),
            pltpu.VMEM((rows, states, LANES), jnp.float32),
        ],
        compiler_params=pltpu.CompilerParams(vmem_limit_bytes=VMEM_LIMIT),
    )(step, drive, up, maps, rate2)


def scan_full(step, drive, up, maps, rate2, rate, entering, leaving, seqs):
    states, width = rate2.shape
    rows = step.shape[0]
    wide = jax.ShapeDtypeStruct((rows, width), jnp.float32)
    return pl.pallas_call(
        partial(scan_kernel, seqs),
        out_shape=(
            wide, wide, wide,
            jax.ShapeDtypeStruct((2 * states, rows), jnp.float32),
            jax.ShapeDtypeStruct((states, width), jnp.float32),
        ),
        in_specs=whole(8),
        out_specs=tuple(whole(5)),
        scratch_shapes=[
            pltpu.VMEM((rows, states, width), jnp.float32),
            pltpu.VMEM((rows, states, LANES), jnp.float32),
            pltpu.VMEM((rows, states, LANES), jnp.float32),
            pltpu.VMEM((rows, states, width), jnp.bfloat16),
            pltpu.VMEM((rows, states, width), jnp.bfloat16),
        ],
        compiler_params=pltpu.CompilerParams(vmem_limit_bytes=VMEM_LIMIT),
    )(step, drive, up, maps, rate2, rate, entering, leaving)


def body(
    inputs,
    lengths,
    out_grad,
    norm_gain,
    input_projection_weight,
    conv_weight,
    conv_bias,
    x_weight,
    dt_weight,
    dt_bias,
    log_decay,
    skip_gain,
    output_projection_weight,
):
    seq_count, local_len, shard_width = inputs.shape
    low_rank = dt_weight.shape[0]
    tap_count = conv_weight.shape[0]
    positions = lax.axis_index("seq") * local_len + jnp.arange(local_len, dtype=jnp.int32)
    token_mask = (positions[None, :] < lengths[:, None]).astype(jnp.float32)[:, :, None]
    full_in, full_gain = (
        lax.all_gather(inputs, "chan", axis=2, tiled=True),
        lax.all_gather(norm_gain, "chan", axis=0, tiled=True),
    )
    full_vals = full_in.astype(jnp.float32)
    model_width = full_vals.shape[2]
    root_scale = lax.rsqrt(jnp.mean(full_vals * full_vals, axis=2, keepdims=True) + epsilon)
    gain_vals = full_gain.astype(jnp.float32)
    normalized_rows = (full_vals * root_scale * gain_vals).astype(jnp.bfloat16)
    projected_xz = jnp.einsum(
        "zim,fmn->fzin",
        normalized_rows,
        input_projection_weight,
        preferred_element_type=jnp.float32,
    )
    inner_act = projected_xz[0].astype(jnp.bfloat16) * token_mask.astype(jnp.bfloat16)
    gate_pre = projected_xz[1]
    left_rim = from_behind(inner_act[:, local_len - tap_count + 1 :], "seq", 1)
    padded = jnp.concatenate([left_rim, inner_act], axis=1).astype(jnp.float32)
    conv_pre = conv_bias + sum(
        (
            conv_weight[offset] * padded[:, offset : offset + local_len]
            for offset in range(tap_count)
        )
    )
    activated = jax.nn.silu(conv_pre).astype(jnp.bfloat16)
    all_act, all_rows = (
        lax.all_gather(activated, "chan", axis=2, tiled=True),
        lax.all_gather(x_weight, "chan", axis=1, tiled=True),
    )
    projected = jnp.einsum("sle,re->slr", all_act, all_rows, preferred_element_type=jnp.float32)
    delta_low = projected[:, :, :low_rank].astype(jnp.bfloat16)
    step_pre = (
        jnp.einsum("slr,re->sle", delta_low, dt_weight, preferred_element_type=jnp.float32)
        + dt_bias
    )
    step_size = jax.nn.softplus(step_pre)
    decay_rate = -jnp.exp(log_decay)
    act_vals = activated.astype(jnp.float32)
    width = step_size.shape[2]
    rate2 = decay_rate * LOG2E
    flat = lambda values: values.reshape(seq_count * local_len, values.shape[-1])
    step_rows = flat(step_size)
    drive_rows = flat(step_size * act_vals)
    maps = flat(projected[:, :, low_rank:]).T
    gate_act = jax.nn.silu(gate_pre)
    grad_full = lax.all_gather(out_grad, "chan", axis=2, tiled=True)
    cotangent_rows = grad_full * token_mask.astype(jnp.bfloat16)
    mixer_output_gradient = jnp.einsum(
        "gtb,rb->gtr", cotangent_rows, output_projection_weight, preferred_element_type=jnp.float32
    )
    grad_scanned = mixer_output_gradient * gate_act
    up_rows = flat(grad_scanned)
    ends, leaves = scan_summary(step_rows, drive_rows, up_rows, maps, rate2, seq_count)
    entering, leaving = carried_in(jnp.sum(step_size, axis=1), rate2, ends, leaves)
    scanned, first_sum, second_sum, maps_grad, rate_sum = scan_full(
        step_rows, drive_rows, up_rows, maps, rate2, decay_rate, entering, leaving, seq_count
    )
    unflat = lambda values: values.reshape(seq_count, local_len, values.shape[-1])
    scanned, first_sum, second_sum = (unflat(part) for part in (scanned, first_sum, second_sum))
    with_skip = scanned + skip_gain * act_vals
    mixer_activation = (with_skip * gate_act).astype(jnp.bfloat16)
    partial_out = jnp.einsum(
        "soj,jp->sop",
        mixer_activation,
        output_projection_weight,
        preferred_element_type=jnp.float32,
    )
    reduced = lax.psum_scatter(partial_out, "chan", scatter_dimension=2, tiled=True)
    mixed_out = (inputs.astype(jnp.float32) + reduced).astype(jnp.bfloat16)
    grad_out_weight = jnp.einsum(
        "bzw,bzy->wy", mixer_activation, cotangent_rows, preferred_element_type=jnp.float32
    )
    grad_gate = (mixer_output_gradient * with_skip * silu_slope(gate_pre)).astype(jnp.bfloat16)
    grad_skip_gain = jnp.sum(grad_scanned * act_vals, axis=(0, 1))
    grad_step = first_sum + act_vals * second_sum
    grad_act = step_size * second_sum + grad_scanned * skip_gain
    maps_grad_rows = unflat(maps_grad.T)
    grad_log_decay = rate_sum * decay_rate
    grad_step_pre = grad_step * jax.nn.sigmoid(step_pre)
    grad_dt_bias = jnp.sum(grad_step_pre, axis=(0, 1))
    grad_step_low = grad_step_pre.astype(jnp.bfloat16)
    grad_dt_weight = jnp.einsum(
        "slr,sle->re", delta_low, grad_step_low, preferred_element_type=jnp.float32
    )
    grad_low_part = jnp.einsum(
        "sle,re->slr", grad_step_low, dt_weight, preferred_element_type=jnp.float32
    )
    partial_grads = jnp.concatenate([grad_low_part, maps_grad_rows], axis=2)
    grad_projected = lax.psum(partial_grads, "chan").astype(jnp.bfloat16)
    grad_x_weight = jnp.einsum(
        "slr,sle->re", grad_projected, activated, preferred_element_type=jnp.float32
    )
    grad_act = grad_act + jnp.einsum(
        "slr,re->sle", grad_projected, x_weight, preferred_element_type=jnp.float32
    )
    grad_conv = (grad_act * silu_slope(conv_pre)).astype(jnp.bfloat16)
    grad_conv_vals = grad_conv.astype(jnp.float32)
    grad_conv_bias = jnp.sum(grad_conv_vals, axis=(0, 1))
    grad_conv_weight = jnp.stack(
        [
            jnp.sum(grad_conv_vals * padded[:, offset : offset + local_len], axis=(0, 1))
            for offset in range(tap_count)
        ]
    )
    next_rim = from_behind(grad_conv[:, : tap_count - 1], "seq", -1)
    extended = jnp.concatenate([grad_conv, next_rim], axis=1).astype(jnp.float32)
    grad_inner_vals = sum(
        (
            conv_weight[offset]
            * extended[:, tap_count - 1 - offset : tap_count - 1 - offset + local_len]
            for offset in range(tap_count)
        )
    )
    grad_inner = (grad_inner_vals * token_mask).astype(jnp.bfloat16)
    inner_gate_gradient = jnp.stack([grad_inner, grad_gate])
    grad_in_weight = jnp.einsum(
        "gpt,vgpr->vtr", normalized_rows, inner_gate_gradient, preferred_element_type=jnp.float32
    )
    grad_normed_part = jnp.einsum(
        "wrvc,wic->rvi",
        inner_gate_gradient,
        input_projection_weight,
        preferred_element_type=jnp.float32,
    )
    chan_index = lax.axis_index("chan")
    grad_normed = lax.psum(grad_normed_part, "chan")
    weighted = grad_normed * gain_vals
    moment = jnp.sum(weighted * full_vals, axis=2, keepdims=True)
    full_back = (
        root_scale * weighted
        - full_vals * (root_scale * root_scale * root_scale) * moment / model_width
    )
    grad_norm_part = lax.dynamic_slice_in_dim(full_back, chan_index * shard_width, shard_width, 2)
    gain_full = jnp.sum(grad_normed * full_vals * root_scale, axis=(0, 1))
    grad_norm_gain = lax.dynamic_slice_in_dim(gain_full, chan_index * shard_width, shard_width, 0)
    grad_inputs = (out_grad.astype(jnp.float32) * token_mask + grad_norm_part).astype(jnp.bfloat16)
    summed = lax.psum(
        (
            grad_norm_gain,
            grad_in_weight,
            grad_conv_weight,
            grad_conv_bias,
            grad_x_weight,
            grad_dt_weight,
            grad_dt_bias,
            grad_log_decay,
            grad_skip_gain,
            grad_out_weight,
        ),
        "seq",
    )
    return (
        mixed_out,
        grad_inputs,
        summed[0],
        summed[1],
        summed[2],
        summed[3],
        summed[4],
        summed[5],
        summed[6],
        summed[7],
        summed[8],
        summed[9],
    )


def solution(mesh):
    in_specs = (
        P(None, "seq", "chan"),
        P(),
        P(None, "seq", "chan"),
        P("chan"),
        P(None, None, "chan"),
        P(None, "chan"),
        P("chan"),
        P(None, "chan"),
        P(None, "chan"),
        P("chan"),
        P(None, "chan"),
        P("chan"),
        P("chan", None),
    )
    out_specs = (
        P(None, "seq", "chan"),
        P(None, "seq", "chan"),
        P("chan"),
        P(None, None, "chan"),
        P(None, "chan"),
        P("chan"),
        P(None, "chan"),
        P(None, "chan"),
        P("chan"),
        P(None, "chan"),
        P("chan"),
        P("chan", None),
    )
    return jax.shard_map(body, mesh=mesh, in_specs=in_specs, out_specs=out_specs, check_vma=False)
```

profile of v0, /device:TPU:0, one launch (start us, length us, event | category | flops | bytes accessed | tf_op | source)
XLA Modules:
  0.0 535.2 jit_solution(9474670512864927506)
XLA Ops:
  8.1 6.0 %all-gather.3 = bf16[4,1,256]{2,1,0:T(2,128)(2,1)S(1)} all-gather(bf16[1,1,256]{2,1,0:T(2,128)(2,1)S(1)} %reshape.146), channel_id=1, replica_groups=mesh['seq'=8,'chan'=4] {'chan'}, dimensions={0}, use_global_device_ids=true | all-gather | bytes 2560 | tf_op jit(solution)/shard_map/all_gather | solution.py:299
  14.0 7.9 %all_gather.33 = bf16[2,128,1024]{2,1,0:T(8,128)(2,1)S(1)} all-gather(bf16[2,128,256]{2,1,0:T(8,128)(2,1)} %param.15), channel_id=1, replica_groups=mesh['seq'=8,'chan'=4] {'chan'}, dimensions={2}, use_global_device_ids=true | all-gather | bytes 655360 | tf_op jit(solution)/shard_map/all_gather | solution.py:298
  24.4 3.5 collective-permute-start
  28.0 7.2 %all_gather.37 = bf16[2,128,1024]{2,1,0:T(8,128)(2,1)S(1)} all-gather(bf16[2,128,256]{2,1,0:T(8,128)(2,1)S(1)} %copy-done.12), channel_id=1, replica_groups=mesh['seq'=8,'chan'=4] {'chan'}, dimensions={2}, use_global_device_ids=true | all-gather | bytes 655360 | tf_op jit(solution)/shard_map/all_gather | solution.py:343
  38.0 6.8 %all_gather.36 = bf16[96,2048]{1,0:T(8,128)(2,1)S(1)} all-gather(bf16[96,512]{1,0:T(8,128)(2,1)} %param.22), channel_id=1, replica_groups=mesh['seq'=8,'chan'=4] {'chan'}, dimensions={1}, use_global_device_ids=true | all-gather | bytes 491520 | tf_op jit(solution)/shard_map/all_gather | solution.py:325
  45.4 9.5 %all-gather.7.cloned.1.call-done = bf16[2,128,2048]{2,1,0:T(8,128)(2,1)} async-done(((bf16[2,128,512]{2,1,0:T(8,128)(2,1)}), bf16[2,128,2048]{2,1,0:T(8,128)(2,1)}) %all-gather.7.cloned.1.call-update) | async-done | bytes 1048592 | tf_op jit(solution)/shard_map/all_gather | solution.py:324
  59.6 30.5 %all-gather.4 = f32[8,2,512]{2,1,0:T(2,128)S(1)} all-gather(f32[1,2,512]{2,1,0:T(2,128)S(1)} %bitcast.146), channel_id=2, replica_groups=mesh['seq'=8,'chan'=4] {'seq'}, dimensions={0}, use_global_device_ids=true | all-gather | bytes 36864 | tf_op jit(solution)/shard_map/all_gather | solution.py:21
  90.9 10.5 %shard_map.220 = (f32[2,16,512]{2,1,0:T(8,128)}, f32[2,16,512]{2,1,0:T(8,128)}) custom-call(f32[256,512]{1,0:T(8,128)} %bitcast.134, f32[256,512]{1,0:T(8,128)} %bitcast.136, f32[256,512]{1,0:T(8,128)} %bitcast.138, f32[32,256]{1,0:T(8,128)} %bitcast_bitcast_fusion.maps_ref, f32[16,512]{1,0:T(8,128)S(1)} %get-tuple-element.408.rate_ref.rate2_ref), custom_call_target="tpu_custom_call" | custom-call | tf_op jit(solution)/shard_map/pallas_call | solution.py:239
  101.4 33.6 %all-gather.1 = f32[16,16,512]{2,1,0:T(8,128)} all-gather(f32[2,16,512]{2,1,0:T(8,128)} %get-tuple-element.218), channel_id=3, replica_groups=mesh['seq'=8,'chan'=4] {'seq'}, dimensions={0}, use_global_device_ids=true | all-gather | bytes 589824 | tf_op jit(solution)/shard_map/all_gather | solution.py:21
  135.0 33.6 %all-gather.2 = f32[16,16,512]{2,1,0:T(8,128)} all-gather(f32[2,16,512]{2,1,0:T(8,128)} %get-tuple-element.219), channel_id=4, replica_groups=mesh['seq'=8,'chan'=4] {'seq'}, dimensions={0}, use_global_device_ids=true | all-gather | bytes 589824 | tf_op jit(solution)/shard_map/all_gather | solution.py:21
  168.7 6.9 %while.18 = (s32[]{:T(128)}, f32[2,16,512]{2,1,0:T(8,128)S(1)}, f32[2,16,512]{2,1,0:T(8,128)S(1)}, s32[]{:T(128)}, f32[8,2,512]{2,1,0:T(2,128)S(1)}, /*index=5*/...) while((s32[]{:T(128)}, f32[2,16,512]{2,1,0:T(8,128)S(1)}, ...), condition=%wide.region_3.4_spmd.clone, body=%wide.region_2.3_spmd.clone.sunk | while | flops 196617 | bytes 450777 | solution.py:35
  175.6 22.5 %shard_map.221 = (f32[256,512]{1,0:T(8,128)}, f32[256,512]{1,0:T(8,128)}, f32[256,512]{1,0:T(8,128)}, f32[32,256]{1,0:T(8,128)}, f32[16,512]{1,0:T(8,128)}) custom-call(f32[256,512]{1,0:T(8,128)} %bitcast.135, f32[256,512]{1,0:T(8,128)} %bitcast.137, f32[256,512]{1,0:T(8,128)} %bitcast.139, f32[32,256]{1,0:T(8,128)} %bitcast_bitcast_fusion.maps_ref, ...), custom_call_target="tpu_custom_call" | custom-call | tf_op jit(solution)/shard_map/pallas_call | solution.py:257
  198.1 3.0 fusion.64
  202.7 12.5 %psum.84 = bf16[2,128,96]{1,2,0:T(8,128)(2,1)} all-reduce(f32[2,128,96]{1,2,0:T(8,128)} %pad_maximum_fusion.3), channel_id=1, replica_groups=mesh['seq'=8,'chan'=4] {'chan'}, use_global_device_ids=true, to_apply=%region_5.6 | all-reduce | flops 24576 | bytes 147456 | tf_op jit(solution)/shard_map/psum | solution.py:386
  215.2 3.5 fusion.22
  220.1 4.2 collective-permute-done.1
  226.8 2.7 fusion.14
  233.0 3.0 convolution_bitcast_fusion.1
  236.0 2.9 convolution_bitcast_fusion
  240.1 20.8 %all-reduce.5.cloned.1.call-done = f32[2,128,1024]{2,1,0:T(8,128)} async-done(((f32[2,128,1024]{2,1,0:T(8,128)}), f32[2,128,1024]{2,1,0:T(8,128)}) %all-reduce.5.cloned.1.call-update) | async-done | bytes 1048592 | tf_op jit(solution)/shard_map/psum | solution.py:423
  263.5 38.1 %all-reduce = (f32[256]{0:T(256)}, f32[4,512]{1,0:T(4,128)}, f32[512]{0:T(512)}, f32[512]{0:T(512)}, f32[16,512]{1,0:T(8,128)}, /*index=5*/f32[512]{0:T(512)}) all-reduce(f32[256]{0:T(256)S(1)} %dynamic_slice.47, f32[4,512]{1,0:T(4,128)S(1)} %pad_maximum_fusion.4, ...), channel_id=1, replica_groups=mesh['seq'=8,'chan'=4] {'seq'}, use_global_device_ids=true, to_apply=%region_9.10 | all-reduce | flops 12032 | bytes 96256 | tf_op jit(solution)/shard_map/psum | solution.py:434
  305.2 213.6 %all-reduce.7.cloned.1.call-done = (f32[2,1024,512]{1,2,0:T(8,128)}, f32[96,512]{1,0:T(8,128)}, f32[64,512]{1,0:T(8,128)}, f32[512,1024]{1,0:T(8,128)}) async-done(((f32[2,1024,512]{1,2,0:T(8,128)}, f32[96,512]{1,0:T(8,128)}, f32[64,512]{1,0:T(8,128)}, f32[512,1024]{1,0:T(8,128)}), (f32[2,1024,512]{1,2,0:T(8,128)}, f32[96,512]{1,0:T(8,128)}, f32[64,512]{1,0:T(8,128)}, ...) | async-done | bytes 6619152 | tf_op jit(solution)/shard_map/psum | solution.py:434
  518.7 5.4 %copy.38 = f32[2,1024,512]{2,1,0:T(8,128)} copy(f32[2,1024,512]{1,2,0:T(8,128)} %get-tuple-element.307) | data formatting | bytes 8388608
  525.5 3.2 copy.71
  (141 shorter events, 36.2 us)
Async XLA Ops:
  7.2 16.3 %copy-start = (bf16[2,1024,512]{2,1,0:T(8,128)(2,1)S(1)}, bf16[2,1024,512]{2,1,0:T(8,128)(2,1)}, u32[]{:S(2)}) copy-start(bf16[2,1024,512]{2,1,0:T(8,128)(2,1)} %param.19) | copy-start | bytes 6291460
  7.2 47.8 %all-gather.7.cloned.1.call-start = ((), (), s32[]{:S(2)}) async-start(), calls=%async_computation.1 | async-start | bytes 1310720 | tf_op jit(solution)/shard_map/all_gather | solution.py:324
  23.4 11.8 %copy-start.31 = (bf16[2,128]{1,0:T(2,128)(2,1)}, bf16[2,128]{1,0:T(2,128)(2,1)S(1)}, u32[]{:S(2)}) copy-start(bf16[2,128]{1,0:T(2,128)(2,1)S(1)} %get-tuple-element.337) | copy-start | bytes 1540
  23.5 11.8 %copy-start.10 = (bf16[512,1024]{1,0:T(8,128)(2,1)S(1)}, bf16[512,1024]{1,0:T(8,128)(2,1)}, u32[]{:S(2)}) copy-start(bf16[512,1024]{1,0:T(8,128)(2,1)} %param.27) | copy-start | bytes 3145732
  23.5 11.8 %copy-start.38 = (f32[512]{0:T(512)S(1)}, f32[512]{0:T(512)}, u32[]{:S(2)}) copy-start(f32[512]{0:T(512)} %param.21) | copy-start | bytes 6148
  24.2 13.6 %copy-start.6 = (f32[2,2,128,512]{3,2,0,1:T(8,128)}, f32[2,2,128,512]{3,2,0,1:T(8,128)S(1)}, u32[]{:S(2)}) copy-start(f32[2,2,128,512]{3,2,0,1:T(8,128)S(1)} %fusion.6) | copy-start | bytes 3145732
  24.4 10.8 %collective-permute-start = (bf16[2,3,512]{2,1,0:T(4,128)(2,1)S(1)}, bf16[2,3,512]{2,1,0:T(4,128)(2,1)S(1)}, u32[]{:S(2)}, u32[]{:S(2)}) collective-permute-start(bf16[2,3,512]{2,1,0:T(4,128)(2,1)S(1)} %slice.83), channel_id=1, source_target_pairs={{0,4},{4,8},{8,12},{12,16},{16,20},{20,24},{24,28},{1,5},{5,9},{9,... | collective-permute-start | bytes 18440 | tf_op jit(solution)/shard_map/ppermute | solution.py:15
  27.9 9.9 %copy-start.23 = (f32[1,512]{1,0:T(1,128)}, f32[1,512]{1,0:T(1,128)S(1)}, u32[]{:S(2)}) copy-start(f32[1,512]{1,0:T(1,128)S(1)} %get-tuple-element.330) | copy-start | bytes 6148
  28.0 9.9 %copy-start.25 = (f32[1,512]{1,0:T(1,128)}, f32[1,512]{1,0:T(1,128)S(1)}, u32[]{:S(2)}) copy-start(f32[1,512]{1,0:T(1,128)S(1)} %get-tuple-element.331) | copy-start | bytes 6148
  28.0 9.9 %copy-start.27 = (f32[1,512]{1,0:T(1,128)}, f32[1,512]{1,0:T(1,128)S(1)}, u32[]{:S(2)}) copy-start(f32[1,512]{1,0:T(1,128)S(1)} %get-tuple-element.332) | copy-start | bytes 6148
  37.9 19.4 %copy-start.35 = (f32[512]{0:T(512)S(1)}, f32[512]{0:T(512)}, u32[]{:S(2)}) copy-start(f32[512]{0:T(512)} %param.24) | copy-start | bytes 6148
  37.9 52.1 %copy-start.5 = (bf16[2,128,512]{2,1,0:T(8,128)(2,1)S(1)}, bf16[2,128,512]{2,1,0:T(8,128)(2,1)}, u32[]{:S(2)}) copy-start(bf16[2,128,512]{2,1,0:T(8,128)(2,1)} %get-tuple-element.313) | copy-start | bytes 786436
  37.9 223.0 %all-reduce.5.cloned.1.call-start = ((), (), s32[]{:S(2)}) async-start(), calls=%async_computation.3 | async-start | bytes 2097152 | tf_op jit(solution)/shard_map/psum | solution.py:423
  59.6 31.4 %copy-start.1 = (f32[2,128,512]{2,1,0:T(8,128)}, f32[2,128,512]{2,1,0:T(8,128)S(1)}, u32[]{:S(2)}) copy-start(f32[2,128,512]{2,1,0:T(8,128)S(1)} %get-tuple-element.319) | copy-start | bytes 1572868
  168.7 29.4 %copy-start.34 = (f32[512]{0:T(512)S(1)}, f32[512]{0:T(512)}, u32[]{:S(2)}) copy-start(f32[512]{0:T(512)} %param.26) | copy-start | bytes 6148
  175.6 22.5 %copy-start.4 = (f32[2,128,512]{2,1,0:T(8,128)S(1)}, f32[2,128,512]{2,1,0:T(8,128)}, u32[]{:S(2)}) copy-start(f32[2,128,512]{2,1,0:T(8,128)} %copy-done.3) | copy-start | bytes 1572868
  198.1 17.1 %copy-start.2 = (f32[2,128,512]{2,1,0:T(8,128)S(1)}, f32[2,128,512]{2,1,0:T(8,128)}, u32[]{:S(2)}) copy-start(f32[2,128,512]{2,1,0:T(8,128)} %copy-done.1) | copy-start | bytes 1572868
  218.7 5.7 %collective-permute-start.1 = (bf16[2,3,512]{2,1,0:T(4,128)(2,1)S(1)}, bf16[2,3,512]{2,1,0:T(4,128)(2,1)S(1)}, u32[]{:S(2)}, u32[]{:S(2)}) collective-permute-start(bf16[2,3,512]{2,1,0:T(4,128)(2,1)S(1)} %slice.91), channel_id=1, source_target_pairs={{4,0},{8,4},{12,8},{16,12},{20,16},{24,20},{28,24},{5,1},{9,5},{13... | collective-permute-start | bytes 18440 | tf_op jit(solution)/shard_map/ppermute | solution.py:15
  226.6 77.0 %reduce-scatter.2.cloned.1.call-start = ((), (), s32[]{:S(2)}) async-start(), calls=%async_computation.2 | async-start | bytes 1310720 | tf_op jit(solution)/shard_map/reduce_scatter | solution.py:365
  229.6 289.2 %all-reduce.7.cloned.1.call-start = ((), (), s32[]{:S(2)}) async-start(), calls=%async_computation.4 | async-start | bytes 13238272 | tf_op jit(solution)/shard_map/psum | solution.py:434
  238.9 24.6 %copy-start.36 = (f32[512]{0:T(512)S(1)}, f32[512]{0:T(512)}, u32[]{:S(2)}) copy-start(f32[512]{0:T(512)} %get-tuple-element.311) | copy-start | bytes 6148
  238.9 62.7 %copy-start.13 = (bf16[2,128,256]{2,1,0:T(8,128)(2,1)S(1)}, bf16[2,128,256]{2,1,0:T(8,128)(2,1)}, u32[]{:S(2)}) copy-start(bf16[2,128,256]{2,1,0:T(8,128)(2,1)} %param.17) | copy-start | bytes 393220
  238.9 62.7 %copy-start.33 = (f32[2,128]{1,0:T(2,128)S(1)}, f32[2,128]{1,0:T(2,128)}, u32[]{:S(2)}) copy-start(f32[2,128]{1,0:T(2,128)} %get-tuple-element.334) | copy-start | bytes 3076
  240.0 63.5 %copy-start.14 = (bf16[2,128,256]{2,1,0:T(8,128)(2,1)S(1)}, bf16[2,128,256]{2,1,0:T(8,128)(2,1)}, u32[]{:S(2)}) copy-start(bf16[2,128,256]{2,1,0:T(8,128)(2,1)} %param.15) | copy-start | bytes 393220
  (21 other events, 107.3 us)
Sparse Core Ops, SparseCore 0:
  38.1 16.8 all-gather.6
  226.7 34.1 all-reduce.4
  263.6 25.2 reduce-scatter.1
  294.4 224.3 all-reduce.6
where the time goes:
time: 536 us; the launch traced here: 535 us
  waiting for transfers between devices  248 us (46%)
  blocking collectives  176 us (33%)
  Pallas kernels  33 us (6%)
  matrix products  23.6 us (4%)
  other arithmetic  21.2 us (4%)
  between operations  14.3 us (3%)
  local copies, waits for them, and re-layouts  13.1 us (2%)
    psum x1, waiting for transfers between devices, body(): lax.psum((grad_norm_gain, grad_in_weight, grad_conv_weight, grad_conv_bia...  214 us
    all_gather x3, blocking collectives, carried_in(): lax.all_gather(part, 'seq')  97.8 us
    psum x1, blocking collectives, body(): lax.psum((grad_norm_gain, grad_in_weight, grad_conv_weight, grad_conv_bia...  38.1 us
    pallas_call x1, Pallas kernels, scan_full(): pl.pallas_call(partial(scan_kernel, seqs), out_shape=(wide, wide, wide, j...  22.5 us
    psum x1, waiting for transfers between devices, body(): grad_normed = lax.psum(grad_normed_part, 'chan')  20.8 us
    psum x1, blocking collectives, body(): grad_projected = lax.psum(partial_grads, 'chan').astype(jnp.bfloat16)  12.5 us
    unnamed x83, local copies, waits for them, and re-layouts  12.4 us
  transfers between devices with their start and end apart: 6, of which 4 were waited for; matrix products, arithmetic and copies ran while one was open for 4% of the time, Pallas kernels for 0%

commit v1 on v0

v1 whole, which is shorter than its diff:
```python
from functools import partial
from types import SimpleNamespace

import jax
import jax.numpy as jnp
from jax import lax
from jax.experimental import pallas as pl
from jax.experimental.pallas import tpu as pltpu
from jax.sharding import PartitionSpec as P

EPSILON = 1e-05
LANES = 128
LOG2E = 1.4426950408889634
VMEM_LIMIT = 60 * 2**20
HALO = 16
MESH = pl.DeviceIdType.MESH
F32 = jnp.float32
BF16 = jnp.bfloat16


def lane_chunks(width):
    return [slice(k * LANES, (k + 1) * LANES) for k in range(width // LANES)]


def flip(index, bit):
    return index + bit - 2 * bit * lax.rem(lax.div(index, bit), 2)


def dot(a, b, contract=((1,), (0,))):
    return lax.dot_general(a, b, (contract, ((), ())), preferred_element_type=F32)


def silu_slope(values, sigmoid):
    return sigmoid * (1.0 + values * (1.0 - sigmoid))


def softplus(values):
    return jnp.maximum(values, 0.0) + jnp.log1p(jnp.exp(-jnp.abs(values)))


def spread_maps(maps, b_ref, c_ref, first, tokens):
    states = maps.shape[0] // 2

    def block(index, _):
        start = index * 8
        rolled = pltpu.roll(maps, lax.rem(tokens - start, tokens), 1)
        for j in range(8):
            column = jnp.broadcast_to(rolled[:, j : j + 1], (2 * states, LANES))
            b_ref[first + start + j] = column[:states]
            c_ref[first + start + j] = column[states:]
        return 0

    lax.fori_loop(0, tokens // 8, block, 0)


def zero_states(rate_ref):
    states, width = rate_ref.shape
    return tuple(jnp.zeros((states, LANES), F32) for _ in lane_chunks(width))


def local_states(decay_ref, step_ref, drive_ref, b_ref, rate_ref, first, tokens):
    chunks = lane_chunks(rate_ref.shape[1])

    def block(index, held):
        held = list(held)
        rows = pl.ds(pl.multiple_of(first + index * 8, 8), 8)
        steps = [step_ref[rows, lanes] for lanes in chunks]
        drives = [drive_ref[rows, lanes] for lanes in chunks]
        for j in range(8):
            token = first + index * 8 + j
            b = b_ref[token]
            for k, lanes in enumerate(chunks):
                decay = jnp.exp2(steps[k][j : j + 1] * rate_ref[:, lanes])
                decay_ref[token, :, lanes] = decay
                held[k] = decay * held[k] + drives[k][j : j + 1] * b
        return tuple(held)

    return lax.fori_loop(0, tokens // 8, block, zero_states(rate_ref))


def local_adjoints(decay_ref, up_ref, c_ref, rate_ref, first, tokens):
    chunks = lane_chunks(rate_ref.shape[1])

    def block(index, held):
        held = list(held)
        start = first + (tokens // 8 - 1 - index) * 8
        rows = pl.ds(pl.multiple_of(start, 8), 8)
        ups = [up_ref[rows, lanes] for lanes in chunks]
        for j in range(7, -1, -1):
            token = start + j
            c = c_ref[token]
            for k, lanes in enumerate(chunks):
                adjoint = c * ups[k][j : j + 1] + held[k]
                held[k] = decay_ref[token, :, lanes] * adjoint
        return tuple(held)

    return lax.fori_loop(0, tokens // 8, block, zero_states(rate_ref))


def run_states(decay_ref, drive_ref, b_ref, c_ref, enter_ref, state_ref, out_ref, which, first, tokens):
    chunks = lane_chunks(decay_ref.shape[2])

    def block(index, held):
        held = list(held)
        rows = pl.ds(pl.multiple_of(first + index * 8, 8), 8)
        drives = [drive_ref[rows, lanes] for lanes in chunks]
        outs = [[] for _ in chunks]
        for j in range(8):
            token = first + index * 8 + j
            b, c = b_ref[token], c_ref[token]
            for k, lanes in enumerate(chunks):
                held[k] = decay_ref[token, :, lanes] * held[k] + drives[k][j : j + 1] * b
                state_ref[token, :, lanes] = held[k].astype(BF16)
                outs[k].append(jnp.sum(c * held[k], axis=0, keepdims=True))
        for k, lanes in enumerate(chunks):
            out_ref[rows, lanes] = jnp.concatenate(outs[k], axis=0)
        return tuple(held)

    lax.fori_loop(0, tokens // 8, block, tuple(enter_ref[which, :, lanes] for lanes in chunks))


def run_adjoints(
    decay_ref, step_ref, up_ref, b_ref, c_ref, rate_ref, enter_ref, state_ref, adjoint_ref,
    first_sum_ref, second_sum_ref, which, first, tokens, span, carried,
):
    chunks = lane_chunks(rate_ref.shape[1])

    def block(index, carried):
        held, total = list(carried[0]), list(carried[1])
        ones = [[None] * 8 for _ in chunks]
        twos = [[None] * 8 for _ in chunks]
        start = first + (tokens // 8 - 1 - index) * 8
        rows = pl.ds(pl.multiple_of(start, 8), 8)
        ups = [up_ref[rows, lanes] for lanes in chunks]
        steps = [step_ref[rows, lanes] for lanes in chunks]
        for j in range(7, -1, -1):
            token = start + j
            b, c = b_ref[token], c_ref[token]
            for k, lanes in enumerate(chunks):
                adjoint = c * ups[k][j : j + 1] + held[k]
                adjoint_ref[token, :, lanes] = adjoint.astype(BF16)
                held[k] = decay_ref[token, :, lanes] * adjoint
                if j > 0:
                    before = state_ref[token - 1, :, lanes].astype(F32)
                else:
                    before = state_ref[jnp.maximum(token - 1, first), :, lanes].astype(F32)
                    before = jnp.where(token == first, enter_ref[which, :, lanes], before)
                pulled = held[k] * before
                ones[k][j] = jnp.sum(pulled * rate_ref[:, lanes], axis=0, keepdims=True)
                twos[k][j] = jnp.sum(adjoint * b, axis=0, keepdims=True)
                total[k] = total[k] + pulled * steps[k][j : j + 1]
        for k, lanes in enumerate(chunks):
            first_sum_ref[rows, lanes] = jnp.concatenate(ones[k], axis=0)
            second_sum_ref[rows, lanes] = jnp.concatenate(twos[k], axis=0)
        return tuple(held), tuple(total)

    return lax.fori_loop(span[0], span[1], block, carried)


def map_sums(values_ref, rows, states, first, tokens):
    width = rows.shape[1]
    flat = values_ref[first : first + tokens].reshape(tokens * states, width)
    all_pairs = dot(flat, rows.astype(BF16), ((1,), (1,)))
    row_token = lax.broadcasted_iota(jnp.int32, (tokens * states, tokens), 0) // states
    column_token = lax.broadcasted_iota(jnp.int32, (tokens * states, tokens), 1)
    kept = jnp.where(row_token == column_token, all_pairs, 0.0).astype(BF16)
    state = lax.broadcasted_iota(jnp.int32, (states, tokens * states), 0)
    row_state = lax.broadcasted_iota(jnp.int32, (states, tokens * states), 1) % states
    return dot((state == row_state).astype(BF16), kept)


def send(src, dst, send_sem, recv_sem, device):
    copy = pltpu.make_async_remote_copy(
        src_ref=src, dst_ref=dst, send_sem=send_sem, recv_sem=recv_sem,
        device_id=device, device_id_type=MESH,
    )
    copy.start()
    return copy


class ChanGather:
    def __init__(self, src, dst, sems, mine, core_peer, x_peer):
        self.dst, self.sems, self.mine, self.core_peer = (dst, sems, mine, core_peer)
        self.over_x = send(src, dst.at[mine], sems.at[0], sems.at[1], x_peer)
        self.over_core = send(src, dst.at[mine], sems.at[2], sems.at[3], core_peer)

    def relay(self):
        self.over_x.wait_recv()
        block = self.dst.at[flip(self.mine, 2)]
        self.onward = send(block, block, self.sems.at[4], self.sems.at[5], self.core_peer)

    def finish(self):
        self.over_core.wait_recv()
        self.onward.wait_recv()
        for copy in (self.over_x, self.over_core, self.onward):
            copy.wait_send()


class ChanSum:
    def __init__(self, own, first, second, middle, sems, core_peer, x_peer):
        self.own, self.first, self.second, self.middle = (own, first, second, middle)
        self.sems, self.x_peer = (sems, x_peer)
        self.copies = [send(own, first, sems.at[0], sems.at[1], core_peer)]

    def cross(self):
        self.copies[0].wait_recv()
        self.middle[...] = self.own[...] + self.first[...]
        self.copies.append(send(self.middle, self.second, self.sems.at[2], self.sems.at[3], self.x_peer))

    def finish(self):
        self.copies[1].wait_recv()
        for copy in self.copies:
            copy.wait_send()
        return self.middle[...] + self.second[...]


class ChanScatter:
    def __init__(self, blocks, first, second, sems, mine, core_peer, x_peer, extra=None):
        self.blocks, self.first, self.second, self.sems = (blocks, first, second, sems)
        self.mine, self.x_peer, self.extra = (mine, x_peer, extra)
        other = flip(mine, 1)
        self.copies = [
            send(blocks.at[other], first.at[0], sems.at[0], sems.at[1], core_peer),
            send(blocks.at[flip(other, 2)], first.at[1], sems.at[2], sems.at[3], core_peer),
        ]
        if extra is not None:
            self.copies.append(send(extra[0], extra[1], sems.at[6], sems.at[7], core_peer))

    def cross(self):
        for copy in self.copies:
            copy.wait_recv()
        far = flip(self.mine, 2)
        self.blocks[far] = (self.blocks[far].astype(F32) + self.first[1].astype(F32)).astype(BF16)
        self.last = [send(self.blocks.at[far], self.second, self.sems.at[4], self.sems.at[5], self.x_peer)]
        if self.extra is not None:
            own, near, middle, across = self.extra
            middle[...] = own[...] + near[...]
            self.last.append(send(middle, across, self.sems.at[8], self.sems.at[9], self.x_peer))

    def finish(self):
        for copy in self.last:
            copy.wait_recv()
        for copy in self.copies + self.last:
            copy.wait_send()
        total = self.blocks[self.mine].astype(F32) + self.first[0].astype(F32) + self.second[...].astype(F32)
        if self.extra is None:
            return total
        return total, self.extra[2][...] + self.extra[3][...]


class SeqSum:
    def __init__(self, held, landing, full, sems, bits, mine, chan):
        self.held, self.landing, self.full, self.sems, self.bits = (held, landing, full, sems, bits)
        self.mine, self.chan = (mine, chan)
        self.regions = []
        self.copies = []
        start, size, place = (0, held.shape[0], 0)
        for bit in bits:
            half = size // 2
            mine_bit = lax.rem(lax.div(mine, bit), 2)
            keep = pl.multiple_of(start + mine_bit * half, 16)
            give = pl.multiple_of(start + (1 - mine_bit) * half, 16)
            self.regions.append((keep, give, half, place))
            start, size, place = (keep, half, place + half)
        self.step = 0
        self.total = 2 * len(bits)
        self.launch()

    def launch(self):
        step, count = (self.step, len(self.bits))
        sems = (self.sems.at[2 * step], self.sems.at[2 * step + 1])
        if step < count:
            _, give, half, place = self.regions[step]
            src, dst = (self.held.at[pl.ds(give, half)], self.landing.at[pl.ds(place, half)])
            bit = self.bits[step]
        else:
            keep, _, half, _ = self.regions[self.total - 1 - step]
            src = dst = self.full.at[pl.ds(keep, half)]
            bit = self.bits[self.total - 1 - step]
        self.copies.append(send(src, dst, *sems, (flip(self.mine, bit), self.chan)))

    def advance(self):
        if self.step == self.total:
            return
        self.copies[-1].wait_recv()
        if self.step < len(self.bits):
            keep, _, half, place = self.regions[self.step]
            rows = pl.ds(keep, half)
            got = self.landing[pl.ds(place, half)].astype(F32)
            into = self.held if self.step < len(self.bits) - 1 else self.full
            into[rows] = (self.held[rows].astype(F32) + got).astype(BF16)
        self.step += 1
        if self.step < self.total:
            self.launch()

    def finish(self):
        while self.step < self.total:
            self.advance()
        for copy in self.copies:
            copy.wait_send()


def layer_kernel(names, seq_devices, *refs):
    r = SimpleNamespace(**dict(zip(names, refs)))
    x_ref, og_ref, win_ref, wout_ref = (r.inputs, r.out_grad, r.w_in, r.w_out)
    xw_ref, dtw_ref = (r.x_weight, r.dt_weight)
    seqs, tokens, shard = x_ref.shape
    model, width = win_ref.shape[1:]
    states = r.log_decay.shape[0]
    low_rank = dtw_ref.shape[0]
    taps = r.conv_weight.shape[0]
    proj = xw_ref.shape[0]
    me_s, me_c = (lax.axis_index("seq"), lax.axis_index("chan"))
    core_peer, x_peer = ((me_s, flip(me_c, 1)), (me_s, flip(me_c, 2)))
    right, left = (lax.rem(me_s + 1, seq_devices), lax.rem(me_s + seq_devices - 1, seq_devices))
    other_chans = [lax.rem(me_c + k, 4) for k in range(1, 4)]

    barrier = pltpu.get_barrier_semaphore()

    def greet(device):
        pl.semaphore_signal(barrier, inc=1, device_id=device, device_id_type=MESH)

    for chan in other_chans:
        greet((me_s, chan))
        greet((right, chan))
        greet((left, chan))

    def greet_seq(k, _):
        greet((lax.rem(me_s + k, seq_devices), me_c))
        return 0

    lax.fori_loop(1, seq_devices, greet_seq, 0)
    pl.semaphore_wait(barrier, 9 + seq_devices - 1)

    gain_ref = r.gain
    gain_ref[me_c] = jnp.broadcast_to(r.norm_gain[...].astype(F32), (8, shard))
    xg_ref, og_all_ref, halo_ref = (r.x_all, r.og_all, r.halo)
    gather_x = ChanGather(x_ref, xg_ref, r.x_sems, me_c, core_peer, x_peer)
    xg_ref[me_c] = x_ref[...]
    og_all_ref[me_c] = og_ref[...]
    last_rows = x_ref.at[:, pl.ds(tokens - HALO, HALO), :]
    halo_copies = []
    for k in range(4):
        device = (right, lax.rem(me_c + k, 4))
        halo_copies.append(
            send(last_rows, halo_ref.at[me_c], r.halo_send.at[k], r.halo_recv.at[me_c], device)
        )
    gain_copies = []
    for k, chan in enumerate(other_chans):
        gain_copies.append(
            send(gain_ref.at[me_c], gain_ref.at[me_c], r.gain_send.at[k], r.gain_recv.at[me_c], (me_s, chan))
        )
    gather_og = ChanGather(og_ref, og_all_ref, r.og_sems, me_c, core_peer, x_peer)
    gather_x.relay()
    gather_x.finish()

    def wait_block(ref, sem, block):
        pltpu.make_async_remote_copy(
            src_ref=ref.at[block], dst_ref=ref.at[block], send_sem=sem.at[block], recv_sem=sem.at[block],
            device_id=core_peer, device_id_type=MESH,
        ).wait_recv()

    for chan in other_chans:
        wait_block(gain_ref, r.gain_recv, chan)
    for chan in range(4):
        wait_block(halo_ref, r.halo_recv, chan)
    for copy in halo_copies + gain_copies:
        copy.wait_send()

    rate_ref, rate2_ref = (r.rate, r.rate2)
    rate_ref[...] = -jnp.exp(r.log_decay[...])
    rate2_ref[...] = rate_ref[...] * LOG2E

    def mask_of(s, rows, begin):
        positions = me_s * tokens + begin + lax.broadcasted_iota(jnp.int32, (rows, 1), 0)
        return (positions < r.lengths[s]).astype(F32)

    def normalize(blocks):
        squares = sum(jnp.sum(b * b, axis=1, keepdims=True) for b in blocks)
        root = lax.rsqrt(squares * (1.0 / model) + EPSILON)
        return root, [(b * root * gain_ref[q, 0:1]).astype(BF16) for q, b in enumerate(blocks)]

    conv_sum = []
    has_left = (me_s > 0).astype(F32)
    for s in range(seqs):
        mine = pl.ds(s * tokens, tokens)
        root, rows = normalize([xg_ref[q, s].astype(F32) for q in range(4)])
        _, before = normalize([halo_ref[q, s].astype(F32) for q in range(4)])
        r.root[mine, :] = jnp.broadcast_to(root, (tokens, LANES))
        normed, normed_before = (jnp.concatenate(rows, axis=1), jnp.concatenate(before, axis=1))
        r.normed[mine, :] = normed
        inner = dot(normed, win_ref[0]).astype(BF16).astype(F32) * mask_of(s, tokens, 0)
        inner_before = dot(normed_before, win_ref[0]).astype(BF16).astype(F32)
        inner_before = inner_before * (mask_of(s, HALO, -HALO) * has_left)
        r.inner[s, HALO:, :] = inner
        r.inner[s, :HALO, :] = inner_before
        conv_pre = r.conv_bias[...] + sum(
            r.conv_weight[k : k + 1, :] * r.inner[s, HALO - taps + 1 + k : HALO - taps + 1 + k + tokens, :]
            for k in range(taps)
        )
        r.conv_pre[mine, :] = conv_pre
        act = (conv_pre * jax.nn.sigmoid(conv_pre)).astype(BF16)
        r.act[mine, :] = act.astype(F32)
        r.proj_own[s] = dot(xw_ref[...], act, ((1,), (1,)))
        conv_sum.append(
            ChanSum(
                r.proj_own.at[s], r.proj_first.at[s], r.proj_second.at[s], r.proj_mid.at[s],
                r.proj_sems.at[s], core_peer, x_peer,
            )
        )
    for s in range(seqs):
        conv_sum[s].cross()
    gather_og.relay()
    for s in range(seqs):
        mine = pl.ds(s * tokens, tokens)
        r.gate_pre[mine, :] = dot(r.normed[mine, :], win_ref[1])
    gather_og.finish()
    for s in range(seqs):
        mine = pl.ds(s * tokens, tokens)
        mask = mask_of(s, tokens, 0).astype(BF16)
        cot = jnp.concatenate([og_all_ref[q, s] * mask for q in range(4)], axis=1)
        r.cot[mine, :] = cot
        grad_mixed = dot(cot, wout_ref[...], ((1,), (1,)))
        gate = r.gate_pre[mine, :]
        r.grad_mixed[mine, :] = grad_mixed
        r.up[mine, :] = grad_mixed * (gate * jax.nn.sigmoid(gate))

    totals_ref = r.totals
    step_totals = []
    for s in range(seqs):
        mine = pl.ds(s * tokens, tokens)
        projected = conv_sum[s].finish()
        low = projected[:low_rank].astype(BF16)
        r.low[:, s * tokens : (s + 1) * tokens] = low
        step_pre = dot(projected[:low_rank].T.astype(BF16), dtw_ref[...]) + r.dt_bias[...]
        r.step_pre[mine, :] = step_pre
        step = softplus(step_pre)
        r.step[mine, :] = step
        r.drive[mine, :] = step * r.act[mine, :]
        step_totals.append(jnp.sum(step, axis=0, keepdims=True))
        spread_maps(projected[low_rank:], r.b, r.c, s * tokens, tokens)
    totals_ref[me_s] = jnp.concatenate(step_totals + [jnp.zeros((8 - seqs, width), F32)], axis=0)

    def seq_device(k):
        return (k, me_c)

    def totals_copy(k):
        peer = lax.rem(me_s + k, seq_devices)
        return pltpu.make_async_remote_copy(
            src_ref=totals_ref.at[me_s], dst_ref=totals_ref.at[me_s],
            send_sem=r.totals_send.at[k], recv_sem=r.totals_recv.at[me_s],
            device_id=seq_device(peer), device_id_type=MESH,
        )

    def start_totals(k, _):
        totals_copy(k).start()
        return 0

    lax.fori_loop(1, seq_devices, start_totals, 0)

    ends_refs = (r.ends, r.ends_send, r.ends_recv)
    leaves_refs = (r.leaves, r.leaves_send, r.leaves_recv)

    def carried_copy(which, s, peer):
        ref, send_sem, recv_sem = which
        return pltpu.make_async_remote_copy(
            src_ref=ref.at[s, me_s], dst_ref=ref.at[s, me_s],
            send_sem=send_sem.at[s, peer], recv_sem=recv_sem.at[s, me_s],
            device_id=seq_device(peer), device_id_type=MESH,
        )

    def start_carried(which, s, begin, end):
        def start(peer, _):
            carried_copy(which, s, peer).start()
            return 0

        lax.fori_loop(begin, end, start, 0)

    def wait_carried(which, s, begin, end):
        def wait(peer, _):
            carried_copy(which, s, peer).wait_send()
            return 0

        lax.fori_loop(begin, end, wait, 0)

    for s in range(seqs):
        ends = local_states(r.decay, r.step, r.drive, r.b, rate2_ref, s * tokens, tokens)
        for k, lanes in enumerate(lane_chunks(width)):
            r.ends[s, me_s, :, lanes] = ends[k].astype(BF16)
        start_carried(ends_refs, s, me_s + 1, seq_devices)
    for s in range(seqs):
        leaves = local_adjoints(r.decay, r.up, r.c, rate_ref, s * tokens, tokens)
        for k, lanes in enumerate(lane_chunks(width)):
            r.leaves[s, me_s, :, lanes] = leaves[k].astype(BF16)
        start_carried(leaves_refs, s, 0, me_s)

    def wait_totals(k, _):
        peer = lax.rem(me_s + k, seq_devices)
        pltpu.make_async_remote_copy(
            src_ref=totals_ref.at[peer], dst_ref=totals_ref.at[peer],
            send_sem=r.totals_send.at[k], recv_sem=r.totals_recv.at[peer],
            device_id=seq_device(peer), device_id_type=MESH,
        ).wait_recv()
        return 0

    lax.fori_loop(1, seq_devices, wait_totals, 0)

    def combine(which, s, count, place):
        ref, send_sem, recv_sem = which

        def turn(k, held):
            peer = place(k)
            pltpu.make_async_remote_copy(
                src_ref=ref.at[s, peer], dst_ref=ref.at[s, peer],
                send_sem=send_sem.at[s, peer], recv_sem=recv_sem.at[s, peer],
                device_id=seq_device(peer), device_id_type=MESH,
            ).wait_recv()
            total = totals_ref[peer][s : s + 1]
            return jnp.exp2(total * rate2_ref[...]) * held + ref[s, peer].astype(F32)

        return lax.fori_loop(0, count, turn, jnp.zeros((states, width), F32))

    for s in range(seqs):
        mine = pl.ds(s * tokens, tokens)
        r.entering[s] = combine(ends_refs, s, me_s, lambda k: k)
        run_states(
            r.decay, r.drive, r.b, r.c, r.entering, r.state, r.scanned, s, s * tokens, tokens
        )
        gate = r.gate_pre[mine, :]
        sigmoid = jax.nn.sigmoid(gate)
        with_skip = r.scanned[mine, :] + r.skip_gain[...] * r.act[mine, :]
        mixed = (with_skip * (gate * sigmoid)).astype(BF16)
        r.mixed[mine, :] = mixed
        r.grad_gate[mine, :] = (r.grad_mixed[mine, :] * with_skip * silu_slope(gate, sigmoid)).astype(BF16)
    out_part = dot(r.mixed[...], wout_ref[...])
    for q in range(4):
        r.out_blocks[q] = out_part[:, q * shard : (q + 1) * shard].astype(BF16)
    scatter_out = ChanScatter(
        r.out_blocks, r.out_first, r.out_second, r.out_sems, me_c, core_peer, x_peer
    )
    bits = [1 << k for k in range(seq_devices.bit_length() - 1)]
    turned = bits[1:] + bits[:1]
    grad_out = dot(r.mixed[...], r.cot[...], ((0,), (0,))).astype(BF16)
    r.grad_w_out[:width, :] = grad_out[:, : model // 2]
    r.grad_w_out[width:, :] = grad_out[:, model // 2 :]
    sums = [SeqSum(r.grad_w_out, r.land_w_out, r.out_w_out, r.w_out_sems, bits, me_s, me_c)]
    r.grad_w_gate[...] = dot(r.normed[...], r.grad_gate[...], ((0,), (0,))).astype(BF16)
    sums.append(SeqSum(r.grad_w_gate, r.land_w_gate, r.out_w_gate, r.w_gate_sems, turned, me_s, me_c))

    blocks = tokens // 8
    rate_sums = None
    small = r.small
    small[...] = jnp.zeros_like(small)
    low_sum = []
    act_part = []
    for s in range(seqs):
        mine = pl.ds(s * tokens, tokens)
        first = s * tokens
        leaving = combine(leaves_refs, s, seq_devices - 1 - me_s, lambda k: seq_devices - 1 - k)
        carried = (tuple(leaving[:, lanes] for lanes in lane_chunks(width)), zero_states(rate_ref))
        parts = 4
        for part in range(parts):
            carried = run_adjoints(
                r.decay, r.step, r.up, r.b, r.c, rate_ref, r.entering, r.state,
                r.adjoint, r.first_sum, r.second_sum, s, first, tokens,
                (part * blocks // parts, (part + 1) * blocks // parts), carried,
            )
            if s == 0 and part == 0:
                scatter_out.cross()
            elif part % 2 == 1:
                for item in sums:
                    item.advance()
        rate_sums = carried[1] if rate_sums is None else [a + b for a, b in zip(rate_sums, carried[1])]
        act, step, step_pre = (r.act[mine, :], r.step[mine, :], r.step_pre[mine, :])
        second = r.second_sum[mine, :]
        grad_step_pre = (r.first_sum[mine, :] + act * second) * jax.nn.sigmoid(step_pre)
        grad_step_low = grad_step_pre.astype(BF16)
        r.grad_step_low[mine, :] = grad_step_low
        small[proj + low_rank + states + taps + 1, :] += jnp.sum(grad_step_pre, axis=0)
        small[proj + low_rank + states + taps + 2, :] += jnp.sum(r.up[mine, :] * act, axis=0)
        r.grad_act[mine, :] = step * second + r.up[mine, :] * r.skip_gain[...]
        own = r.proj_own.at[s]
        own[:low_rank, :] = dot(dtw_ref[...], grad_step_low, ((1,), (1,)))
        own[low_rank : low_rank + states, :] = map_sums(r.adjoint, r.drive[mine, :], states, first, tokens)
        own[low_rank + states :, :] = map_sums(r.state, r.up[mine, :], states, first, tokens)
        low_sum.append(
            ChanSum(
                own, r.back_first.at[s], r.back_second.at[s], r.back_mid.at[s],
                r.back_sems.at[s], core_peer, x_peer,
            )
        )
        if s > 0:
            low_sum[s - 1].cross()
    out_sum = scatter_out.finish()
    for s in range(seqs):
        r.mixed_out[s] = (x_ref[s].astype(F32) + out_sum[s * tokens : (s + 1) * tokens]).astype(BF16)
    low_sum[seqs - 1].cross()
    for k, lanes in enumerate(lane_chunks(width)):
        small[proj + low_rank : proj + low_rank + states, lanes] = rate_sums[k] * rate_ref[:, lanes]
    small[proj : proj + low_rank, :] = dot(r.low[...], r.grad_step_low[...])
    for item in sums:
        item.advance()

    rim_copies = []
    for s in range(seqs):
        mine = pl.ds(s * tokens, tokens)
        grad_projected = low_sum[s].finish()
        r.grad_proj[:, s * tokens : (s + 1) * tokens] = grad_projected.astype(BF16)
        grad_act = r.grad_act[mine, :] + dot(grad_projected.T.astype(BF16), xw_ref[...])
        conv_pre = r.conv_pre[mine, :]
        grad_conv = (grad_act * silu_slope(conv_pre, jax.nn.sigmoid(conv_pre))).astype(BF16)
        r.rim_own[s] = grad_conv[:HALO]
        r.grad_conv[s, :tokens, :] = grad_conv.astype(F32)
        rim_copies.append(
            send(r.rim_own.at[s], r.rim.at[s], r.rim_sems.at[2 * s], r.rim_sems.at[2 * s + 1], (left, me_c))
        )
        small[proj + low_rank + states + taps, :] += jnp.sum(grad_conv.astype(F32), axis=0)
        for k in range(taps):
            shifted = r.inner[s, HALO - taps + 1 + k : HALO - taps + 1 + k + tokens, :]
            small[proj + low_rank + states + k, :] += jnp.sum(grad_conv.astype(F32) * shifted, axis=0)
    small[:proj, :] = dot(r.grad_proj[...], r.act[...].astype(BF16))
    for item in sums:
        item.advance()
    has_right = (me_s < seq_devices - 1).astype(F32)
    for s in range(seqs):
        mine = pl.ds(s * tokens, tokens)
        rim_copies[s].wait_recv()
        rim_copies[s].wait_send()
        r.grad_conv[s, tokens:, :] = r.rim[s].astype(F32) * has_right
        grad_inner = sum(
            r.conv_weight[k : k + 1, :] * r.grad_conv[s, taps - 1 - k : taps - 1 - k + tokens, :]
            for k in range(taps)
        )
        r.grad_inner[mine, :] = (grad_inner * mask_of(s, tokens, 0)).astype(BF16)

    late = r.grad_w_inner
    late[:model, :] = dot(r.normed[...], r.grad_inner[...], ((0,), (0,))).astype(BF16)
    late[model:, :] = small[...].astype(BF16)
    sums.append(SeqSum(late, r.land_w_inner, r.out_w_inner, r.w_inner_sems, bits, me_s, me_c))
    moment = None
    for q in range(4):
        cols = pl.ds(q * shard, shard)
        part = dot(r.grad_inner[...], win_ref[0, q * shard : (q + 1) * shard, :], ((1,), (1,)))
        part = part + dot(r.grad_gate[...], win_ref[1, q * shard : (q + 1) * shard, :], ((1,), (1,)))
        values = xg_ref[q].reshape(seqs * tokens, shard).astype(F32)
        term = jnp.sum(part * gain_ref[q, 0:1] * values, axis=1, keepdims=True)
        moment = term if moment is None else moment + term
        r.gn_blocks[q] = part.astype(BF16)
    r.moment[...] = jnp.broadcast_to(moment, (seqs * tokens, LANES)).T[:8]
    scatter_gn = ChanScatter(
        r.gn_blocks, r.gn_first, r.gn_second, r.gn_sems, me_c, core_peer, x_peer,
        (r.moment, r.moment_first, r.moment_mid, r.moment_second),
    )
    for item in sums:
        item.advance()
    scatter_gn.cross()
    for item in sums:
        item.advance()
    grad_normed, moment_row = scatter_gn.finish()
    moment = jnp.broadcast_to(moment_row[:1], (LANES, seqs * tokens)).T[:, :1]
    root = r.root[:, :1]
    values = x_ref[...].reshape(seqs * tokens, shard).astype(F32)
    gains = r.norm_gain[...].astype(F32)
    back = root * (grad_normed * gains) - values * (root * root * root) * moment * (1.0 / model)
    for s in range(seqs):
        mine = slice(s * tokens, (s + 1) * tokens)
        cot = og_ref[s].astype(F32) * mask_of(s, tokens, 0)
        r.grad_inputs[s] = (cot + back[mine]).astype(BF16)
    gain_sums_ref = r.gain_sums
    gain_sums_ref[me_s] = jnp.broadcast_to(jnp.sum(grad_normed * values * root, axis=0, keepdims=True), (8, shard))

    def gain_copy(k):
        peer = lax.rem(me_s + k, seq_devices)
        return pltpu.make_async_remote_copy(
            src_ref=gain_sums_ref.at[me_s], dst_ref=gain_sums_ref.at[me_s],
            send_sem=r.gain_sums_send.at[k], recv_sem=r.gain_sums_recv.at[me_s],
            device_id=seq_device(peer), device_id_type=MESH,
        )

    def start_gain(k, _):
        gain_copy(k).start()
        return 0

    lax.fori_loop(1, seq_devices, start_gain, 0)
    for step in range(max(item.total for item in sums)):
        for item in sums:
            item.advance()

    def take_gain(k, _):
        peer = lax.rem(me_s + k, seq_devices)
        pltpu.make_async_remote_copy(
            src_ref=gain_sums_ref.at[peer], dst_ref=gain_sums_ref.at[peer],
            send_sem=r.gain_sums_send.at[k], recv_sem=r.gain_sums_recv.at[peer],
            device_id=seq_device(peer), device_id_type=MESH,
        ).wait_recv()
        gain_copy(k).wait_send()
        totals_copy(k).wait_send()
        return 0

    lax.fori_loop(1, seq_devices, take_gain, 0)
    r.grad_gain[...] = jnp.sum(gain_sums_ref[...], axis=0)
    for item in sums:
        item.finish()
    for s in range(seqs):
        wait_carried(ends_refs, s, me_s + 1, seq_devices)
        wait_carried(leaves_refs, s, 0, me_s)


def layer(
    seq_devices,
    inputs, lengths, out_grad, norm_gain, w_in, conv_weight, conv_bias, x_weight, dt_weight,
    dt_bias, log_decay, skip_gain, w_out,
):
    seqs, tokens, shard = inputs.shape
    _, model, width = w_in.shape
    states, low_rank, taps, proj = (log_decay.shape[0], dt_weight.shape[0], conv_weight.shape[0], x_weight.shape[0])
    rows = seqs * tokens
    small_rows = proj + low_rank + states + taps + 3
    grain = 16 * seq_devices
    small_rows = -(-small_rows // grain) * grain
    steps = 4 * (seq_devices.bit_length() - 1)
    dma = pltpu.SemaphoreType.DMA
    vmem = pltpu.VMEM
    operands = dict(
        inputs=inputs, lengths=lengths, out_grad=out_grad, norm_gain=norm_gain.reshape(1, shard),
        w_in=w_in, conv_weight=conv_weight, conv_bias=conv_bias.reshape(1, width),
        x_weight=x_weight, dt_weight=dt_weight, dt_bias=dt_bias.reshape(1, width),
        log_decay=log_decay, skip_gain=skip_gain.reshape(1, width), w_out=w_out,
    )
    outputs = dict(
        mixed_out=(inputs.shape, BF16), grad_inputs=(inputs.shape, BF16), grad_gain=((8, shard), F32),
        out_w_out=((2 * width, model // 2), BF16), out_w_gate=((model, width), BF16),
        out_w_inner=((model + small_rows, width), BF16),
    )
    wide = (rows, width)
    scratch = dict(
        x_all=vmem((4,) + inputs.shape, BF16), og_all=vmem((4,) + inputs.shape, BF16),
        halo=vmem((4, seqs, HALO, shard), BF16), gain=vmem((4, 8, shard), F32),
        x_sems=dma((6,)), og_sems=dma((6,)), halo_send=dma((4,)), halo_recv=dma((4,)),
        gain_send=dma((3,)), gain_recv=dma((4,)),
        rate=vmem((states, width), F32), rate2=vmem((states, width), F32),
        root=vmem((rows, LANES), F32), normed=vmem((rows, model), BF16),
        inner=vmem((seqs, HALO + tokens, width), F32),
        conv_pre=vmem(wide, F32), act=vmem(wide, F32), gate_pre=vmem(wide, F32),
        cot=vmem((rows, model), BF16), grad_mixed=vmem(wide, F32), up=vmem(wide, F32),
        proj_own=vmem((seqs, proj, tokens), F32), proj_first=vmem((seqs, proj, tokens), F32),
        proj_second=vmem((seqs, proj, tokens), F32), proj_mid=vmem((seqs, proj, tokens), F32),
        proj_sems=dma((seqs, 4)),
        back_first=vmem((seqs, proj, tokens), F32), back_second=vmem((seqs, proj, tokens), F32),
        back_mid=vmem((seqs, proj, tokens), F32), back_sems=dma((seqs, 4)),
        low=vmem((low_rank, rows), BF16), step_pre=vmem(wide, F32), step=vmem(wide, F32),
        drive=vmem(wide, F32), b=vmem((rows, states, LANES), F32), c=vmem((rows, states, LANES), F32),
        decay=vmem((rows, states, width), F32),
        totals=vmem((seq_devices, 8, width), F32), totals_send=dma((seq_devices,)),
        totals_recv=dma((seq_devices,)),
        ends=vmem((seqs, seq_devices, states, width), BF16), ends_send=dma((seqs, seq_devices)),
        ends_recv=dma((seqs, seq_devices)),
        leaves=vmem((seqs, seq_devices, states, width), BF16), leaves_send=dma((seqs, seq_devices)),
        leaves_recv=dma((seqs, seq_devices)),
        entering=vmem((seqs, states, width), F32),
        state=vmem((rows, states, width), BF16), adjoint=vmem((rows, states, width), BF16),
        scanned=vmem(wide, F32), first_sum=vmem(wide, F32), second_sum=vmem(wide, F32),
        mixed=vmem(wide, BF16), grad_gate=vmem(wide, BF16), grad_step_low=vmem(wide, BF16),
        grad_act=vmem(wide, F32), grad_proj=vmem((proj, rows), BF16),
        grad_conv=vmem((seqs, tokens + HALO, width), F32), rim_own=vmem((seqs, HALO, width), BF16),
        rim=vmem((seqs, HALO, width), BF16), rim_sems=dma((2 * seqs,)),
        grad_inner=vmem(wide, BF16),
        out_blocks=vmem((4, rows, shard), BF16), out_first=vmem((2, rows, shard), BF16),
        out_second=vmem((rows, shard), BF16), out_sems=dma((6,)),
        gn_blocks=vmem((4, rows, shard), BF16), gn_first=vmem((2, rows, shard), BF16),
        gn_second=vmem((rows, shard), BF16), gn_sems=dma((10,)),
        moment=vmem((8, rows), F32), moment_first=vmem((8, rows), F32),
        moment_mid=vmem((8, rows), F32), moment_second=vmem((8, rows), F32),
        small=vmem((small_rows, width), F32),
        grad_w_out=vmem((2 * width, model // 2), BF16), land_w_out=vmem((2 * width, model // 2), BF16),
        w_out_sems=dma((steps,)),
        grad_w_gate=vmem((model, width), BF16), land_w_gate=vmem((model, width), BF16),
        w_gate_sems=dma((steps,)),
        grad_w_inner=vmem((model + small_rows, width), BF16),
        land_w_inner=vmem((model + small_rows, width), BF16), w_inner_sems=dma((steps,)),
        gain_sums=vmem((seq_devices, 8, shard), F32), gain_sums_send=dma((seq_devices,)),
        gain_sums_recv=dma((seq_devices,)),
    )
    names = list(operands) + list(outputs) + list(scratch)
    spaces = dict(lengths=pltpu.SMEM)
    mixed_out, grad_inputs, gain, w_out_grad, w_gate_grad, late = pl.pallas_call(
        partial(layer_kernel, names, seq_devices),
        out_shape=tuple(jax.ShapeDtypeStruct(*item) for item in outputs.values()),
        in_specs=[pl.BlockSpec(memory_space=spaces.get(name, pltpu.VMEM)) for name in operands],
        out_specs=tuple(pl.BlockSpec(memory_space=pltpu.VMEM) for _ in outputs),
        scratch_shapes=list(scratch.values()),
        compiler_params=pltpu.CompilerParams(
            collective_id=0, has_side_effects=True, vmem_limit_bytes=VMEM_LIMIT
        ),
    )(*operands.values())
    grad_w_out = jnp.concatenate([w_out_grad[:width], w_out_grad[width:]], axis=1).astype(F32)
    grad_w_in = jnp.stack([late[:model], w_gate_grad]).astype(F32)
    small = late[model:].astype(F32)
    at = proj + low_rank + states
    return (
        mixed_out, grad_inputs, gain[0], grad_w_in, small[at : at + taps], small[at + taps],
        small[:proj], small[proj : proj + low_rank], small[at + taps + 1],
        small[proj + low_rank : at], small[at + taps + 2], grad_w_out,
    )


def solution(mesh):
    in_specs = (
        P(None, "seq", "chan"), P(), P(None, "seq", "chan"), P("chan"), P(None, None, "chan"),
        P(None, "chan"), P("chan"), P(None, "chan"), P(None, "chan"), P("chan"), P(None, "chan"),
        P("chan"), P("chan", None),
    )
    out_specs = (
        P(None, "seq", "chan"), P(None, "seq", "chan"), P("chan"), P(None, None, "chan"),
        P(None, "chan"), P("chan"), P(None, "chan"), P(None, "chan"), P("chan"), P(None, "chan"),
        P("chan"), P("chan", None),
    )
    body = partial(layer, mesh.shape["seq"])
    return jax.shard_map(body, mesh=mesh, in_specs=in_specs, out_specs=out_specs, check_vma=False)
```

time: 536 us -> 179 us (0.33)
  waiting for transfers between devices: 248 us -> 0 us
  blocking collectives: 176 us -> 0 us
  Pallas kernels: 33 us -> 164 us
  matrix products: 23.6 us -> 0 us
  other arithmetic: 21.2 us -> 4.96 us
  between operations: 14.3 us -> 0.71 us
    psum x2 -> x0, waiting for transfers between devices: 234 us -> none  [the longest x1 214 us: body(): lax.psum((grad_norm_gain, grad_in_weight, grad_conv_weight, grad_conv_bia...]
    pallas_call x2 -> x1, Pallas kernels: 33 us -> 164 us  [layer(): pl.pallas_call(partial(layer_kernel, names, seq_devices), out_shape=tuple...]
    all_gather x7 -> x0, blocking collectives: 126 us -> none  [the longest x3 97.8 us: carried_in(): lax.all_gather(part, 'seq')]
    psum x2 -> x0, blocking collectives: 50.6 us -> none  [the longest x1 38.1 us: body(): lax.psum((grad_norm_gain, grad_in_weight, grad_conv_weight, grad_conv_bia...]
    dot_general x12 -> x0, matrix products: 23.6 us -> none  [the longest x1 3.49 us: body(): jnp.einsum('slr,re->sle', grad_projected, x_weight, preferred_element_typ...]
    unnamed x83 -> x10, local copies, waits for them, and re-layouts: 12.4 us -> 1.33 us
    all_gather x1 -> x0, waiting for transfers between devices: 9.55 us -> none  [body(): lax.all_gather(activated, 'chan', axis=2, tiled=True)]
    select_n x7 -> x0, other arithmetic: 6.57 us -> none  [turn(): jnp.where(later > mine, backward, leaving)]
  transfers between devices with their start and end apart: 6 -> 0, of which waited for: 4 -> 0; matrix products, arithmetic and copies ran while one was open for 4% -> 0% of each run, Pallas kernels for 0% -> 0%
where the time goes in v1:
time: 179 us; the launch traced here: 178 us
  Pallas kernels  164 us (92%)
  local copies, waits for them, and re-layouts  8.42 us (5%)
  other arithmetic  4.96 us (3%)
    pallas_call x1, Pallas kernels, layer(): pl.pallas_call(partial(layer_kernel, names, seq_devices), out_shape=tuple...  164 us

profile of v1, /device:TPU:0, one launch (start us, length us, event | category | flops | bytes accessed | tf_op | source)
XLA Modules:
  0.0 178.4 jit_solution(16062963928880182557)
XLA Ops:
  0.6 1.2 reshape.36.refs_3_
  1.9 164.4 %shard_map.220 = (bf16[2,128,256]{2,1,0:T(8,128)(2,1)}, bf16[2,128,256]{2,1,0:T(8,128)(2,1)}, f32[8,256]{1,0:T(8,128)}, bf16[1024,512]{1,0:T(8,128)(2,1)}, bf16[...) custom-call(bf16[2,128,256]{2,1,0:T(8,128)(2,1)} %refs_0_.1, s32[2]{0:T(128)} %refs_1_.1, bf16[2,128,256]{2,1,0:T(8,128)(2,1)} %refs_2_.1, ...), custom_call_target="tpu_custom_call" | custom-call | tf_op jit(solution)/shard_map/pallas_call | solution.py:786
  166.2 0.0 copy-start.1
  166.2 1.3 slice.36
  167.6 1.3 slice_bitcast_fusion
  168.9 0.0 copy-done.1
  168.9 2.3 %maximum_convert_fusion = f32[2,1024,512]{2,1,0:T(8,128)} fusion(bf16[1,1024,512]{2,1,0:T(8,128)(2,1)S(1)} %bitcast.10, bf16[1,1024,512]{2,1,0:T(8,128)(2,1)S(1)} %slice_bitcast_fusion), kind=kLoop, calls=%fused_computation | loop fusion | flops 2097152 | bytes 6291456 | tf_op jit(solution)/shard_map/convert_element_type | solution.py:797
  171.2 0.0 copy-start
  171.2 1.1 slice_convert_fusion
  172.3 0.6 slice.48
  172.9 0.6 fusion.1
  173.5 0.7 slice.50
  174.2 0.7 slice.51
  174.8 0.6 slice.53
  175.4 0.0 copy-done
  175.4 0.1 fusion
  175.5 0.0 copy-start.3
  175.5 0.0 copy-start.2
  175.5 1.6 maximum_convert_fusion.1
  177.1 0.0 copy-done.3
  177.1 0.7 copy.27
  177.8 0.0 copy-done.2
  177.8 0.7 copy.28
Async XLA Ops:
  166.2 2.7 %copy-start.1 = (bf16[1024,512]{1,0:T(8,128)(2,1)S(1)}, bf16[1024,512]{1,0:T(8,128)(2,1)}, u32[]{:S(2)}) copy-start(bf16[1024,512]{1,0:T(8,128)(2,1)} %get-tuple-element.22) | copy-start | bytes 3145732
  171.2 4.3 %copy-start = (bf16[1024,512]{1,0:T(8,128)(2,1)S(1)}, bf16[1024,512]{1,0:T(8,128)(2,1)}, u32[]{:S(2)}) copy-start(bf16[1024,512]{1,0:T(8,128)(2,1)} %get-tuple-element.23) | copy-start | bytes 3145732
  175.5 1.6 copy-start.3
  175.5 2.3 %copy-start.2 = (bf16[2,128,256]{2,1,0:T(8,128)(2,1)S(1)}, bf16[2,128,256]{2,1,0:T(8,128)(2,1)}, u32[]{:S(2)}) copy-start(bf16[2,128,256]{2,1,0:T(8,128)(2,1)} %get-tuple-element.42) | copy-start | bytes 393220

commit v2 on v1

--- a/solution.py
+++ b/solution.py
@@ -13,6 +13,7 @@
 LOG2E = 1.4426950408889634
 VMEM_LIMIT = 60 * 2**20
 HALO = 16
+MOST_GATHERED = 8
 MESH = pl.DeviceIdType.MESH
 F32 = jnp.float32
 BF16 = jnp.bfloat16
@@ -113,7 +114,7 @@
                 state_ref[token, :, lanes] = held[k].astype(BF16)
                 outs[k].append(jnp.sum(c * held[k], axis=0, keepdims=True))
         for k, lanes in enumerate(chunks):
-            out_ref[rows, lanes] = jnp.concatenate(outs[k], axis=0)
+            out_ref[pl.ds(pl.multiple_of(index * 8, 8), 8), lanes] = jnp.concatenate(outs[k], axis=0)
         return tuple(held)
 
     lax.fori_loop(0, tokens // 8, block, tuple(enter_ref[which, :, lanes] for lanes in chunks))
@@ -138,7 +139,7 @@
             b, c = b_ref[token], c_ref[token]
             for k, lanes in enumerate(chunks):
                 adjoint = c * ups[k][j : j + 1] + held[k]
-                adjoint_ref[token, :, lanes] = adjoint.astype(BF16)
+                adjoint_ref[token - first, :, lanes] = adjoint.astype(BF16)
                 held[k] = decay_ref[token, :, lanes] * adjoint
                 if j > 0:
                     before = state_ref[token - 1, :, lanes].astype(F32)
@@ -149,9 +150,10 @@
                 ones[k][j] = jnp.sum(pulled * rate_ref[:, lanes], axis=0, keepdims=True)
                 twos[k][j] = jnp.sum(adjoint * b, axis=0, keepdims=True)
                 total[k] = total[k] + pulled * steps[k][j : j + 1]
+        own_rows = pl.ds(pl.multiple_of(start - first, 8), 8)
         for k, lanes in enumerate(chunks):
-            first_sum_ref[rows, lanes] = jnp.concatenate(ones[k], axis=0)
-            second_sum_ref[rows, lanes] = jnp.concatenate(twos[k], axis=0)
+            first_sum_ref[own_rows, lanes] = jnp.concatenate(ones[k], axis=0)
+            second_sum_ref[own_rows, lanes] = jnp.concatenate(twos[k], axis=0)
         return tuple(held), tuple(total)
 
     return lax.fori_loop(span[0], span[1], block, carried)
@@ -179,14 +181,14 @@
 
 
 class ChanGather:
-    def __init__(self, src, dst, sems, mine, core_peer, x_peer):
-        self.dst, self.sems, self.mine, self.core_peer = (dst, sems, mine, core_peer)
-        self.over_x = send(src, dst.at[mine], sems.at[0], sems.at[1], x_peer)
-        self.over_core = send(src, dst.at[mine], sems.at[2], sems.at[3], core_peer)
+    def __init__(self, src, place, sems, mine, core_peer, x_peer):
+        self.place, self.sems, self.mine, self.core_peer = (place, sems, mine, core_peer)
+        self.over_x = send(src, place(mine), sems.at[0], sems.at[1], x_peer)
+        self.over_core = send(src, place(mine), sems.at[2], sems.at[3], core_peer)
 
     def relay(self):
         self.over_x.wait_recv()
-        block = self.dst.at[flip(self.mine, 2)]
+        block = self.place(flip(self.mine, 2))
         self.onward = send(block, block, self.sems.at[4], self.sems.at[5], self.core_peer)
 
     def finish(self):
@@ -194,6 +196,94 @@
         self.onward.wait_recv()
         for copy in (self.over_x, self.over_core, self.onward):
             copy.wait_send()
+
+
+def ring_position(index, count):
+    return lax.div(index, 2) + lax.rem(index, 2) * (count - 1 - 2 * lax.div(index, 2))
+
+
+def ring_device(position, count):
+    position = lax.rem(position + 2 * count, count)
+    back = lax.div(position, count // 2)
+    return 2 * position + back * (2 * (count - 1 - position) + 1 - 2 * position)
+
+
+class RingGather:
+    def __init__(self, place, sems, count, mine, chan, more_left):
+        self.place, self.sems, self.count, self.chan = (place, sems, count, chan)
+        self.position = ring_position(mine, count)
+        most = count // 2
+        self.steps = (most, count - 1 - most) if more_left else (count - 1 - most, most)
+        self.length = most
+        self.copies = []
+        self.step = 0
+        self.launch()
+
+    def source(self, side, step):
+        return ring_device(self.position + (step if side else -step), self.count)
+
+    def launch(self):
+        for side in range(2):
+            if self.step < self.steps[side]:
+                block = self.place(self.source(side, self.step))
+                towards = ring_device(self.position + (-1 if side else 1), self.count)
+                sems = self.sems.at[side, self.step]
+                self.copies.append(send(block, block, sems.at[0], sems.at[1], (towards, self.chan)))
+
+    def advance(self):
+        if self.step == self.length:
+            return []
+        arrived = []
+        for side in range(2):
+            if self.step < self.steps[side]:
+                source = self.source(side, self.step + 1)
+                block = self.place(source)
+                sems = self.sems.at[side, self.step]
+                pltpu.make_async_remote_copy(
+                    src_ref=block, dst_ref=block, send_sem=sems.at[0], recv_sem=sems.at[1],
+                    device_id=(source, self.chan), device_id_type=MESH,
+                ).wait_recv()
+                arrived.append(source)
+        self.step += 1
+        self.launch()
+        return arrived
+
+    def finish(self):
+        while self.step < self.length:
+            self.advance()
+        for copy in self.copies:
+            copy.wait_send()
+
+
+class GridGather:
+    def __init__(self, place, ring_sems, chan_sems, count, me_s, me_c, core_peer, x_peer):
+        self.place, self.mine, self.sems = (place, me_c, chan_sems)
+        self.peers = (core_peer, x_peer)
+        self.ring = RingGather(lambda d: place(me_c, d), ring_sems, count, me_s, me_c, True)
+        self.gathers = []
+        self.relayed = 0
+
+    def advance(self):
+        for source in self.ring.advance():
+            self.gathers.append(
+                ChanGather(
+                    self.place(self.mine, source), partial(self.at, source), self.sems.at[len(self.gathers)],
+                    self.mine, *self.peers,
+                )
+            )
+
+    def at(self, source, chan):
+        return self.place(chan, source)
+
+    def relay(self, upto):
+        while self.relayed < min(upto, len(self.gathers)):
+            self.gathers[self.relayed].relay()
+            self.relayed += 1
+
+    def finish(self):
+        self.ring.finish()
+        for gather in self.gathers:
+            gather.finish()
 
 
 class ChanSum:
@@ -313,59 +403,59 @@
     me_s, me_c = (lax.axis_index("seq"), lax.axis_index("chan"))
     core_peer, x_peer = ((me_s, flip(me_c, 1)), (me_s, flip(me_c, 2)))
     right, left = (lax.rem(me_s + 1, seq_devices), lax.rem(me_s + seq_devices - 1, seq_devices))
-    other_chans = [lax.rem(me_c + k, 4) for k in range(1, 4)]
+    position = ring_position(me_s, seq_devices)
+    gathered = seq_devices <= MOST_GATHERED
+    spot = me_s if gathered else 0
 
     barrier = pltpu.get_barrier_semaphore()
 
-    def greet(device):
-        pl.semaphore_signal(barrier, inc=1, device_id=device, device_id_type=MESH)
-
-    for chan in other_chans:
-        greet((me_s, chan))
-        greet((right, chan))
-        greet((left, chan))
-
-    def greet_seq(k, _):
-        greet((lax.rem(me_s + k, seq_devices), me_c))
-        return 0
-
-    lax.fori_loop(1, seq_devices, greet_seq, 0)
-    pl.semaphore_wait(barrier, 9 + seq_devices - 1)
-
-    gain_ref = r.gain
-    gain_ref[me_c] = jnp.broadcast_to(r.norm_gain[...].astype(F32), (8, shard))
-    xg_ref, og_all_ref, halo_ref = (r.x_all, r.og_all, r.halo)
-    gather_x = ChanGather(x_ref, xg_ref, r.x_sems, me_c, core_peer, x_peer)
-    xg_ref[me_c] = x_ref[...]
-    og_all_ref[me_c] = og_ref[...]
-    last_rows = x_ref.at[:, pl.ds(tokens - HALO, HALO), :]
-    halo_copies = []
-    for k in range(4):
-        device = (right, lax.rem(me_c + k, 4))
-        halo_copies.append(
-            send(last_rows, halo_ref.at[me_c], r.halo_send.at[k], r.halo_recv.at[me_c], device)
+    def greet(semaphore, device):
+        pl.semaphore_signal(semaphore, inc=1, device_id=device, device_id_type=MESH)
+
+    ring = [(ring_device(position + step, seq_devices), me_c) for step in (1, -1)]
+    first_peers = [core_peer, x_peer, (right, me_c), (left, me_c)] + ring
+    for device in first_peers:
+        greet(barrier, device)
+    pl.semaphore_wait(barrier, len(first_peers))
+
+    xo_ref, halo_ref = (r.xo, r.halo)
+    gather_x = ChanGather(x_ref, lambda q: xo_ref.at[q, spot, 0], r.x_sems, me_c, core_peer, x_peer)
+    halo_copy = send(
+        x_ref.at[:, pl.ds(tokens - HALO, HALO), :], halo_ref.at[me_c, pl.ds(0, seqs)],
+        r.halo_sems.at[6], r.halo_sems.at[7], (right, me_c),
+    )
+    for device in ring:
+        greet(r.known.at[0], device)
+    gather_og = ChanGather(og_ref, lambda q: xo_ref.at[q, spot, 1], r.og_sems, me_c, core_peer, x_peer)
+    xo_ref[me_c, spot, 0] = x_ref[...]
+    xo_ref[me_c, spot, 1] = og_ref[...]
+    halo_ref[me_c, seqs] = jnp.broadcast_to(r.norm_gain[...], (HALO, shard))
+    if gathered:
+        gather_all = GridGather(
+            lambda q, d: xo_ref.at[q, d], r.xo_ring_sems, r.xo_chan_sems, seq_devices, me_s, me_c, core_peer, x_peer
         )
-    gain_copies = []
-    for k, chan in enumerate(other_chans):
-        gain_copies.append(
-            send(gain_ref.at[me_c], gain_ref.at[me_c], r.gain_send.at[k], r.gain_recv.at[me_c], (me_s, chan))
-        )
-    gather_og = ChanGather(og_ref, og_all_ref, r.og_sems, me_c, core_peer, x_peer)
+    halo_copy.wait_recv()
+    gather_halo = ChanGather(
+        halo_ref.at[me_c], lambda q: halo_ref.at[q], r.halo_sems, me_c, core_peer, x_peer
+    )
     gather_x.relay()
+    gather_halo.relay()
     gather_x.finish()
-
-    def wait_block(ref, sem, block):
-        pltpu.make_async_remote_copy(
-            src_ref=ref.at[block], dst_ref=ref.at[block], send_sem=sem.at[block], recv_sem=sem.at[block],
-            device_id=core_peer, device_id_type=MESH,
-        ).wait_recv()
-
-    for chan in other_chans:
-        wait_block(gain_ref, r.gain_recv, chan)
-    for chan in range(4):
-        wait_block(halo_ref, r.halo_recv, chan)
-    for copy in halo_copies + gain_copies:
-        copy.wait_send()
+    gather_halo.finish()
+    halo_copy.wait_send()
+    gather_og.relay()
+
+    reaches = [1]
+    while 2 * reaches[-1] < seq_devices // 2:
+        reaches.append(2 * reaches[-1])
+
+    def hear(k):
+        pl.semaphore_wait(r.known.at[k], 2)
+        if k + 1 < len(reaches):
+            for step in (reaches[k + 1], -reaches[k + 1]):
+                greet(r.known.at[k + 1], (ring_device(position + step, seq_devices), me_c))
+
+    hear(0)
 
     rate_ref, rate2_ref = (r.rate, r.rate2)
     rate_ref[...] = -jnp.exp(r.log_decay[...])
@@ -375,20 +465,25 @@
         positions = me_s * tokens + begin + lax.broadcasted_iota(jnp.int32, (rows, 1), 0)
         return (positions < r.lengths[s]).astype(F32)
 
+    def gain_of(q):
+        return halo_ref[q, seqs, 0:1, :].astype(F32)
+
     def normalize(blocks):
         squares = sum(jnp.sum(b * b, axis=1, keepdims=True) for b in blocks)
         root = lax.rsqrt(squares * (1.0 / model) + EPSILON)
-        return root, [(b * root * gain_ref[q, 0:1]).astype(BF16) for q, b in enumerate(blocks)]
+        return root, [(b * root * gain_of(q)).astype(BF16) for q, b in enumerate(blocks)]
 
     conv_sum = []
+    normed_rows = []
     has_left = (me_s > 0).astype(F32)
     for s in range(seqs):
         mine = pl.ds(s * tokens, tokens)
-        root, rows = normalize([xg_ref[q, s].astype(F32) for q in range(4)])
+        root, rows = normalize([xo_ref[q, spot, 0, s].astype(F32) for q in range(4)])
         _, before = normalize([halo_ref[q, s].astype(F32) for q in range(4)])
         r.root[mine, :] = jnp.broadcast_to(root, (tokens, LANES))
         normed, normed_before = (jnp.concatenate(rows, axis=1), jnp.concatenate(before, axis=1))
-        r.normed[mine, :] = normed
+        normed_rows.append(pl.ds(pl.multiple_of(spot * seqs * tokens + s * tokens, tokens), tokens))
+        r.normed[normed_rows[s], :] = normed
         inner = dot(normed, win_ref[0]).astype(BF16).astype(F32) * mask_of(s, tokens, 0)
         inner_before = dot(normed_before, win_ref[0]).astype(BF16).astype(F32)
         inner_before = inner_before * (mask_of(s, HALO, -HALO) * has_left)
@@ -410,20 +505,26 @@
         )
     for s in range(seqs):
         conv_sum[s].cross()
-    gather_og.relay()
     for s in range(seqs):
         mine = pl.ds(s * tokens, tokens)
-        r.gate_pre[mine, :] = dot(r.normed[mine, :], win_ref[1])
+        r.gate_pre[mine, :] = dot(r.normed[normed_rows[s], :], win_ref[1])
     gather_og.finish()
     for s in range(seqs):
         mine = pl.ds(s * tokens, tokens)
-        mask = mask_of(s, tokens, 0).astype(BF16)
-        cot = jnp.concatenate([og_all_ref[q, s] * mask for q in range(4)], axis=1)
-        r.cot[mine, :] = cot
-        grad_mixed = dot(cot, wout_ref[...], ((1,), (1,)))
+        cot = jnp.concatenate([xo_ref[q, spot, 1, s] for q in range(4)], axis=1)
+        grad_mixed = dot(cot, wout_ref[...], ((1,), (1,))) * mask_of(s, tokens, 0)
         gate = r.gate_pre[mine, :]
+        sigmoid = jax.nn.sigmoid(gate)
         r.grad_mixed[mine, :] = grad_mixed
-        r.up[mine, :] = grad_mixed * (gate * jax.nn.sigmoid(gate))
+        r.up[mine, :] = grad_mixed * (gate * sigmoid)
+        if gathered:
+            rows = normed_rows[s]
+            r.gate_act_all[rows, :] = (gate * sigmoid * mask_of(s, tokens, 0)).astype(BF16)
+            r.gate_slope_all[rows, :] = (grad_mixed * silu_slope(gate, sigmoid)).astype(BF16)
+        else:
+            r.cot[mine, :] = (cot.astype(F32) * mask_of(s, tokens, 0)).astype(BF16)
+    if gathered:
+        gather_all.advance()
 
     totals_ref = r.totals
     step_totals = []
@@ -456,6 +557,8 @@
         totals_copy(k).start()
         return 0
 
+    for k in range(1, len(reaches)):
+        hear(k)
     lax.fori_loop(1, seq_devices, start_totals, 0)
 
     ends_refs = (r.ends, r.ends_send, r.ends_recv)
@@ -488,6 +591,9 @@
         for k, lanes in enumerate(lane_chunks(width)):
             r.ends[s, me_s, :, lanes] = ends[k].astype(BF16)
         start_carried(ends_refs, s, me_s + 1, seq_devices)
+    if gathered:
+        gather_all.advance()
+        gather_all.relay(1)
     for s in range(seqs):
         leaves = local_adjoints(r.decay, r.up, r.c, rate_ref, s * tokens, tokens)
         for k, lanes in enumerate(lane_chunks(width)):
@@ -520,6 +626,26 @@
 
         return lax.fori_loop(0, count, turn, jnp.zeros((states, width), F32))
 
+    skip_gathers, inner_gathers = ([], [])
+
+    def block_of(ref, s, device):
+        return ref.at[device, s]
+
+    def foreign(k, _):
+        device = lax.rem(me_s + k, seq_devices)
+        rows = pl.ds(pl.multiple_of(device * (seqs * tokens), seqs * tokens), seqs * tokens)
+        blocks = [xo_ref[q, device, 0].reshape(seqs * tokens, shard).astype(F32) for q in range(4)]
+        normed = jnp.concatenate(normalize(blocks)[1], axis=1)
+        r.normed[rows, :] = normed
+        gate = dot(normed, win_ref[1])
+        sigmoid = jax.nn.sigmoid(gate)
+        cot = jnp.concatenate([xo_ref[q, device, 1].reshape(seqs * tokens, shard) for q in range(4)], axis=1)
+        mask = jnp.concatenate([mask_of(s, tokens, (device - me_s) * tokens) for s in range(seqs)], axis=0)
+        grad_mixed = dot(cot, wout_ref[...], ((1,), (1,))) * mask
+        r.gate_act_all[rows, :] = (gate * sigmoid * mask).astype(BF16)
+        r.gate_slope_all[rows, :] = (grad_mixed * silu_slope(gate, sigmoid)).astype(BF16)
+        return 0
+
     for s in range(seqs):
         mine = pl.ds(s * tokens, tokens)
         r.entering[s] = combine(ends_refs, s, me_s, lambda k: k)
@@ -528,81 +654,77 @@
         )
         gate = r.gate_pre[mine, :]
         sigmoid = jax.nn.sigmoid(gate)
-        with_skip = r.scanned[mine, :] + r.skip_gain[...] * r.act[mine, :]
+        with_skip = r.scanned[...] + r.skip_gain[...] * r.act[mine, :]
         mixed = (with_skip * (gate * sigmoid)).astype(BF16)
         r.mixed[mine, :] = mixed
         r.grad_gate[mine, :] = (r.grad_mixed[mine, :] * with_skip * silu_slope(gate, sigmoid)).astype(BF16)
+        if gathered:
+            r.skip_all[me_s, s] = with_skip.astype(BF16)
+            skip_gathers.append(
+                RingGather(
+                    partial(block_of, r.skip_all, s), r.skip_sems.at[s], seq_devices, me_s, me_c, s == 0
+                )
+            )
     out_part = dot(r.mixed[...], wout_ref[...])
     for q in range(4):
         r.out_blocks[q] = out_part[:, q * shard : (q + 1) * shard].astype(BF16)
     scatter_out = ChanScatter(
         r.out_blocks, r.out_first, r.out_second, r.out_sems, me_c, core_peer, x_peer
     )
+    sums = []
     bits = [1 << k for k in range(seq_devices.bit_length() - 1)]
     turned = bits[1:] + bits[:1]
-    grad_out = dot(r.mixed[...], r.cot[...], ((0,), (0,))).astype(BF16)
-    r.grad_w_out[:width, :] = grad_out[:, : model // 2]
-    r.grad_w_out[width:, :] = grad_out[:, model // 2 :]
-    sums = [SeqSum(r.grad_w_out, r.land_w_out, r.out_w_out, r.w_out_sems, bits, me_s, me_c)]
-    r.grad_w_gate[...] = dot(r.normed[...], r.grad_gate[...], ((0,), (0,))).astype(BF16)
-    sums.append(SeqSum(r.grad_w_gate, r.land_w_gate, r.out_w_gate, r.w_gate_sems, turned, me_s, me_c))
-
-    blocks = tokens // 8
-    rate_sums = None
+    if gathered:
+        gather_all.advance()
+        gather_all.relay(3)
+    else:
+        r.grad_w_out[...] = dot(r.mixed[...], r.cot[...], ((0,), (0,))).astype(BF16)
+        sums.append(SeqSum(r.grad_w_out, r.land_w_out, r.out_w_out, r.w_out_sems, bits, me_s, me_c))
+        r.grad_w_gate[...] = dot(r.normed[...], r.grad_gate[...], ((0,), (0,))).astype(BF16)
+        sums.append(SeqSum(r.grad_w_gate, r.land_w_gate, r.out_w_in.at[1], r.w_gate_sems, turned, me_s, me_c))
+
     small = r.small
     small[...] = jnp.zeros_like(small)
-    low_sum = []
-    act_part = []
-    for s in range(seqs):
-        mine = pl.ds(s * tokens, tokens)
-        first = s * tokens
+    decay_row = proj + low_rank
+    tap_row = decay_row + states
+    low_sum, rim_copies, rate_sums = ([], [], [])
+    has_right = (me_s < seq_devices - 1).astype(F32)
+
+    def scan_back(s, services):
         leaving = combine(leaves_refs, s, seq_devices - 1 - me_s, lambda k: seq_devices - 1 - k)
         carried = (tuple(leaving[:, lanes] for lanes in lane_chunks(width)), zero_states(rate_ref))
-        parts = 4
-        for part in range(parts):
+        parts, blocks = (len(services), tokens // 8)
+        for part, service in enumerate(services):
             carried = run_adjoints(
                 r.decay, r.step, r.up, r.b, r.c, rate_ref, r.entering, r.state,
-                r.adjoint, r.first_sum, r.second_sum, s, first, tokens,
+                r.adjoint, r.first_sum, r.second_sum, s, s * tokens, tokens,
                 (part * blocks // parts, (part + 1) * blocks // parts), carried,
             )
-            if s == 0 and part == 0:
-                scatter_out.cross()
-            elif part % 2 == 1:
-                for item in sums:
-                    item.advance()
-        rate_sums = carried[1] if rate_sums is None else [a + b for a, b in zip(rate_sums, carried[1])]
+            service()
+        rate_sums.append(carried[1])
+
+    def after_scan(s):
+        mine = pl.ds(s * tokens, tokens)
         act, step, step_pre = (r.act[mine, :], r.step[mine, :], r.step_pre[mine, :])
-        second = r.second_sum[mine, :]
-        grad_step_pre = (r.first_sum[mine, :] + act * second) * jax.nn.sigmoid(step_pre)
+        second = r.second_sum[...]
+        grad_step_pre = (r.first_sum[...] + act * second) * jax.nn.sigmoid(step_pre)
         grad_step_low = grad_step_pre.astype(BF16)
-        r.grad_step_low[mine, :] = grad_step_low
-        small[proj + low_rank + states + taps + 1, :] += jnp.sum(grad_step_pre, axis=0)
-        small[proj + low_rank + states + taps + 2, :] += jnp.sum(r.up[mine, :] * act, axis=0)
-        r.grad_act[mine, :] = step * second + r.up[mine, :] * r.skip_gain[...]
         own = r.proj_own.at[s]
         own[:low_rank, :] = dot(dtw_ref[...], grad_step_low, ((1,), (1,)))
-        own[low_rank : low_rank + states, :] = map_sums(r.adjoint, r.drive[mine, :], states, first, tokens)
-        own[low_rank + states :, :] = map_sums(r.state, r.up[mine, :], states, first, tokens)
+        own[low_rank : low_rank + states, :] = map_sums(r.adjoint, r.drive[mine, :], states, 0, tokens)
+        own[low_rank + states :, :] = map_sums(r.state, r.up[mine, :], states, s * tokens, tokens)
         low_sum.append(
             ChanSum(
                 own, r.back_first.at[s], r.back_second.at[s], r.back_mid.at[s],
                 r.back_sems.at[s], core_peer, x_peer,
             )
         )
-        if s > 0:
-            low_sum[s - 1].cross()
-    out_sum = scatter_out.finish()
-    for s in range(seqs):
-        r.mixed_out[s] = (x_ref[s].astype(F32) + out_sum[s * tokens : (s + 1) * tokens]).astype(BF16)
-    low_sum[seqs - 1].cross()
-    for k, lanes in enumerate(lane_chunks(width)):
-        small[proj + low_rank : proj + low_rank + states, lanes] = rate_sums[k] * rate_ref[:, lanes]
-    small[proj : proj + low_rank, :] = dot(r.low[...], r.grad_step_low[...])
-    for item in sums:
-        item.advance()
-
-    rim_copies = []
-    for s in range(seqs):
+        r.grad_step_low[mine, :] = grad_step_low
+        small[tap_row + taps + 1, :] += jnp.sum(grad_step_pre, axis=0)
+        small[tap_row + taps + 2, :] += jnp.sum(r.up[mine, :] * act, axis=0)
+        r.grad_act[mine, :] = step * second + r.up[mine, :] * r.skip_gain[...]
+
+    def through_conv(s):
         mine = pl.ds(s * tokens, tokens)
         grad_projected = low_sum[s].finish()
         r.grad_proj[:, s * tokens : (s + 1) * tokens] = grad_projected.astype(BF16)
@@ -610,19 +732,17 @@
         conv_pre = r.conv_pre[mine, :]
         grad_conv = (grad_act * silu_slope(conv_pre, jax.nn.sigmoid(conv_pre))).astype(BF16)
         r.rim_own[s] = grad_conv[:HALO]
-        r.grad_conv[s, :tokens, :] = grad_conv.astype(F32)
         rim_copies.append(
             send(r.rim_own.at[s], r.rim.at[s], r.rim_sems.at[2 * s], r.rim_sems.at[2 * s + 1], (left, me_c))
         )
-        small[proj + low_rank + states + taps, :] += jnp.sum(grad_conv.astype(F32), axis=0)
+        grad_conv = grad_conv.astype(F32)
+        r.grad_conv[s, :tokens, :] = grad_conv
+        small[tap_row + taps, :] += jnp.sum(grad_conv, axis=0)
         for k in range(taps):
             shifted = r.inner[s, HALO - taps + 1 + k : HALO - taps + 1 + k + tokens, :]
-            small[proj + low_rank + states + k, :] += jnp.sum(grad_conv.astype(F32) * shifted, axis=0)
-    small[:proj, :] = dot(r.grad_proj[...], r.act[...].astype(BF16))
-    for item in sums:
-        item.advance()
-    has_right = (me_s < seq_devices - 1).astype(F32)
-    for s in range(seqs):
+            small[tap_row + k, :] += jnp.sum(grad_conv * shifted, axis=0)
+
+    def inner_of(s):
         mine = pl.ds(s * tokens, tokens)
         rim_copies[s].wait_recv()
         rim_copies[s].wait_send()
@@ -631,19 +751,64 @@
             r.conv_weight[k : k + 1, :] * r.grad_conv[s, taps - 1 - k : taps - 1 - k + tokens, :]
             for k in range(taps)
         )
-        r.grad_inner[mine, :] = (grad_inner * mask_of(s, tokens, 0)).astype(BF16)
-
-    late = r.grad_w_inner
-    late[:model, :] = dot(r.normed[...], r.grad_inner[...], ((0,), (0,))).astype(BF16)
-    late[model:, :] = small[...].astype(BF16)
-    sums.append(SeqSum(late, r.land_w_inner, r.out_w_inner, r.w_inner_sems, bits, me_s, me_c))
+        grad_inner = (grad_inner * mask_of(s, tokens, 0)).astype(BF16)
+        r.grad_inner[mine, :] = grad_inner
+        if gathered:
+            r.inner_all[me_s, s] = grad_inner
+            inner_gathers.append(
+                RingGather(
+                    partial(block_of, r.inner_all, s), r.inner_sems.at[s], seq_devices, me_s, me_c, s == 0
+                )
+            )
+
+    def all_advance():
+        for item in sums + skip_gathers + inner_gathers:
+            item.advance()
+
+    def grid_advance(upto):
+        if gathered:
+            gather_all.advance()
+            gather_all.relay(upto)
+
+    def nothing():
+        pass
+
+    scan_back(0, (scatter_out.cross, all_advance, partial(grid_advance, 5), all_advance))
+    after_scan(0)
+    scan_back(1, (low_sum[0].cross, all_advance, partial(through_conv, 0), all_advance))
+    after_scan(1)
+    inner_of(0)
+    low_sum[1].cross()
+    if gathered:
+        gather_all.relay(7)
+        gather_all.finish()
+        lax.fori_loop(1, 3, foreign, 0)
+    out_sum = scatter_out.finish()
+    for s in range(seqs):
+        r.mixed_out[s] = (x_ref[s].astype(F32) + out_sum[s * tokens : (s + 1) * tokens]).astype(BF16)
+    through_conv(1)
+    for k, lanes in enumerate(lane_chunks(width)):
+        small[decay_row:tap_row, lanes] = (rate_sums[0][k] + rate_sums[1][k]) * rate_ref[:, lanes]
+    small[proj:decay_row, :] = dot(r.low[...], r.grad_step_low[...])
+    small[:proj, :] = dot(r.grad_proj[...], r.act[...].astype(BF16))
+    for item in sums:
+        item.advance()
+    inner_of(1)
+
+    if gathered:
+        r.grad_small[...] = small[...].astype(BF16)
+        sums.append(SeqSum(r.grad_small, r.land_small, r.out_small, r.small_sems, bits, me_s, me_c))
+    else:
+        late = r.grad_w_inner
+        late[:model, :] = dot(r.normed[...], r.grad_inner[...], ((0,), (0,))).astype(BF16)
+        late[model:, :] = small[...].astype(BF16)
+        sums.append(SeqSum(late, r.land_w_inner, r.full_w_inner, r.w_inner_sems, bits, me_s, me_c))
     moment = None
     for q in range(4):
-        cols = pl.ds(q * shard, shard)
         part = dot(r.grad_inner[...], win_ref[0, q * shard : (q + 1) * shard, :], ((1,), (1,)))
         part = part + dot(r.grad_gate[...], win_ref[1, q * shard : (q + 1) * shard, :], ((1,), (1,)))
-        values = xg_ref[q].reshape(seqs * tokens, shard).astype(F32)
-        term = jnp.sum(part * gain_ref[q, 0:1] * values, axis=1, keepdims=True)
+        values = xo_ref[q, spot, 0].reshape(seqs * tokens, shard).astype(F32)
+        term = jnp.sum(part * gain_of(q) * values, axis=1, keepdims=True)
         moment = term if moment is None else moment + term
         r.gn_blocks[q] = part.astype(BF16)
     r.moment[...] = jnp.broadcast_to(moment, (seqs * tokens, LANES)).T[:8]
@@ -651,11 +816,13 @@
         r.gn_blocks, r.gn_first, r.gn_second, r.gn_sems, me_c, core_peer, x_peer,
         (r.moment, r.moment_first, r.moment_mid, r.moment_second),
     )
-    for item in sums:
-        item.advance()
+    if gathered:
+        lax.fori_loop(3, 5, foreign, 0)
     scatter_gn.cross()
-    for item in sums:
-        item.advance()
+    all_advance()
+    if gathered:
+        lax.fori_loop(5, seq_devices, foreign, 0)
+        all_advance()
     grad_normed, moment_row = scatter_gn.finish()
     moment = jnp.broadcast_to(moment_row[:1], (LANES, seqs * tokens)).T[:, :1]
     root = r.root[:, :1]
@@ -682,9 +849,57 @@
         return 0
 
     lax.fori_loop(1, seq_devices, start_gain, 0)
-    for step in range(max(item.total for item in sums)):
-        for item in sums:
-            item.advance()
+    if gathered:
+        all_advance()
+        for gather in skip_gathers:
+            gather.finish()
+        count = seq_devices * seqs * tokens
+
+        def mix(device, _):
+            rows = pl.ds(pl.multiple_of(device * (seqs * tokens), seqs * tokens), seqs * tokens)
+            with_skip = r.skip_all[device].reshape(seqs * tokens, width).astype(F32)
+            r.gate_act_all[rows, :] = (r.gate_act_all[rows, :].astype(F32) * with_skip).astype(BF16)
+            r.gate_slope_all[rows, :] = (r.gate_slope_all[rows, :].astype(F32) * with_skip).astype(BF16)
+            return 0
+
+        lax.fori_loop(0, seq_devices, mix, 0)
+        results = []
+
+        def deliver(src, dst):
+            copy = pltpu.make_async_copy(src, dst, r.result_sems.at[len(results)])
+            copy.start()
+            results.append(copy)
+
+        staged = r.skip_all.reshape(count, width)
+        for q in range(4):
+            outs = xo_ref[q, :, 1].reshape(count, shard)
+            half, place = (q * shard // width, q * shard % width)
+            rows = pl.ds(half * width, width)
+            staged[rows, place : place + shard] = dot(r.gate_act_all[...], outs, ((0,), (0,))).astype(BF16)
+            if place + shard == width:
+                deliver(staged.at[rows], r.out_w_out.at[:, pl.ds(half * width, width)])
+            all_advance()
+        for q in range(4):
+            rows = slice(q * shard, (q + 1) * shard)
+            r.gate_act_all[rows, :] = dot(r.normed[:, rows], r.gate_slope_all[...], ((0,), (0,))).astype(BF16)
+            all_advance()
+        deliver(r.gate_act_all.at[pl.ds(0, model)], r.out_w_in.at[1])
+        for gather in inner_gathers:
+            gather.finish()
+        inner_rows = r.inner_all[...].reshape(count, width)
+        for q in range(4):
+            rows = slice(model + q * shard, model + (q + 1) * shard)
+            cols = slice(q * shard, (q + 1) * shard)
+            r.gate_act_all[rows, :] = dot(r.normed[:, cols], inner_rows, ((0,), (0,))).astype(BF16)
+            if q % 2 == 1:
+                deliver(
+                    r.gate_act_all.at[pl.ds(model + (q - 1) * shard, 2 * shard)],
+                    r.out_w_in.at[0, pl.ds((q - 1) * shard, 2 * shard)],
+                )
+            all_advance()
+    else:
+        for step in range(max(item.total for item in sums)):
+            all_advance()
 
     def take_gain(k, _):
         peer = lax.rem(me_s + k, seq_devices)
@@ -701,9 +916,41 @@
     r.grad_gain[...] = jnp.sum(gain_sums_ref[...], axis=0)
     for item in sums:
         item.finish()
+    if gathered:
+        for copy in results:
+            copy.wait()
+    else:
+        r.out_w_in[0] = r.full_w_inner[:model, :]
+        r.out_small[...] = r.full_w_inner[model:, :]
     for s in range(seqs):
         wait_carried(ends_refs, s, me_s + 1, seq_devices)
         wait_carried(leaves_refs, s, 0, me_s)
+
+
+def finish_kernel(
+    rows_of, mixed_ref, inputs_ref, w_in_ref, w_out_ref, small_ref, gain_ref,
+    mixed_out, grad_inputs, gain_out, w_in_out, conv_w_out, conv_b_out, x_out, dt_w_out, dt_b_out, decay_out,
+    skip_out, w_out_out,
+):
+    mixed_out[...] = mixed_ref[...]
+    grad_inputs[...] = inputs_ref[...]
+    w_in_out[...] = w_in_ref[...].astype(F32)
+    w_out_out[...] = w_out_ref[...].astype(F32)
+
+    @pl.when(pl.program_id(0) == 0)
+    def _():
+        proj, low_rank, states, taps = rows_of
+        small = small_ref[...].astype(F32)
+        decay_row = proj + low_rank
+        tap_row = decay_row + states
+        gain_out[...] = gain_ref[0:1, :]
+        x_out[...] = small[:proj]
+        dt_w_out[...] = small[proj:decay_row]
+        decay_out[...] = small[decay_row:tap_row]
+        conv_w_out[...] = small[tap_row : tap_row + taps]
+        conv_b_out[...] = small[tap_row + taps : tap_row + taps + 1]
+        dt_b_out[...] = small[tap_row + taps + 1 : tap_row + taps + 2]
+        skip_out[...] = small[tap_row + taps + 2 : tap_row + taps + 3]
 
 
 def layer(
@@ -719,6 +966,7 @@
     grain = 16 * seq_devices
     small_rows = -(-small_rows // grain) * grain
     steps = 4 * (seq_devices.bit_length() - 1)
+    gathered = seq_devices <= MOST_GATHERED
     dma = pltpu.SemaphoreType.DMA
     vmem = pltpu.VMEM
     operands = dict(
@@ -729,20 +977,18 @@
     )
     outputs = dict(
         mixed_out=(inputs.shape, BF16), grad_inputs=(inputs.shape, BF16), grad_gain=((8, shard), F32),
-        out_w_out=((2 * width, model // 2), BF16), out_w_gate=((model, width), BF16),
-        out_w_inner=((model + small_rows, width), BF16),
+        out_w_in=(w_in.shape, BF16), out_w_out=(w_out.shape, BF16), out_small=((small_rows, width), BF16),
     )
     wide = (rows, width)
     scratch = dict(
-        x_all=vmem((4,) + inputs.shape, BF16), og_all=vmem((4,) + inputs.shape, BF16),
-        halo=vmem((4, seqs, HALO, shard), BF16), gain=vmem((4, 8, shard), F32),
-        x_sems=dma((6,)), og_sems=dma((6,)), halo_send=dma((4,)), halo_recv=dma((4,)),
-        gain_send=dma((3,)), gain_recv=dma((4,)),
+        xo=vmem((4, seq_devices if gathered else 1, 2) + inputs.shape, BF16),
+        halo=vmem((4, seqs + 1, HALO, shard), BF16), known=pltpu.SemaphoreType.REGULAR((8,)),
+        x_sems=dma((6,)), og_sems=dma((6,)), halo_sems=dma((8,)),
         rate=vmem((states, width), F32), rate2=vmem((states, width), F32),
-        root=vmem((rows, LANES), F32), normed=vmem((rows, model), BF16),
+        root=vmem((rows, LANES), F32), normed=vmem((seq_devices * rows if gathered else rows, model), BF16),
         inner=vmem((seqs, HALO + tokens, width), F32),
         conv_pre=vmem(wide, F32), act=vmem(wide, F32), gate_pre=vmem(wide, F32),
-        cot=vmem((rows, model), BF16), grad_mixed=vmem(wide, F32), up=vmem(wide, F32),
+        grad_mixed=vmem(wide, F32), up=vmem(wide, F32),
         proj_own=vmem((seqs, proj, tokens), F32), proj_first=vmem((seqs, proj, tokens), F32),
         proj_second=vmem((seqs, proj, tokens), F32), proj_mid=vmem((seqs, proj, tokens), F32),
         proj_sems=dma((seqs, 4)),
@@ -758,8 +1004,9 @@
         leaves=vmem((seqs, seq_devices, states, width), BF16), leaves_send=dma((seqs, seq_devices)),
         leaves_recv=dma((seqs, seq_devices)),
         entering=vmem((seqs, states, width), F32),
-        state=vmem((rows, states, width), BF16), adjoint=vmem((rows, states, width), BF16),
-        scanned=vmem(wide, F32), first_sum=vmem(wide, F32), second_sum=vmem(wide, F32),
+        state=vmem((rows, states, width), BF16), adjoint=vmem((tokens, states, width), BF16),
+        scanned=vmem((tokens, width), F32), first_sum=vmem((tokens, width), F32),
+        second_sum=vmem((tokens, width), F32),
         mixed=vmem(wide, BF16), grad_gate=vmem(wide, BF16), grad_step_low=vmem(wide, BF16),
         grad_act=vmem(wide, F32), grad_proj=vmem((proj, rows), BF16),
         grad_conv=vmem((seqs, tokens + HALO, width), F32), rim_own=vmem((seqs, HALO, width), BF16),
@@ -772,36 +1019,79 @@
         moment=vmem((8, rows), F32), moment_first=vmem((8, rows), F32),
         moment_mid=vmem((8, rows), F32), moment_second=vmem((8, rows), F32),
         small=vmem((small_rows, width), F32),
-        grad_w_out=vmem((2 * width, model // 2), BF16), land_w_out=vmem((2 * width, model // 2), BF16),
-        w_out_sems=dma((steps,)),
-        grad_w_gate=vmem((model, width), BF16), land_w_gate=vmem((model, width), BF16),
-        w_gate_sems=dma((steps,)),
-        grad_w_inner=vmem((model + small_rows, width), BF16),
-        land_w_inner=vmem((model + small_rows, width), BF16), w_inner_sems=dma((steps,)),
         gain_sums=vmem((seq_devices, 8, shard), F32), gain_sums_send=dma((seq_devices,)),
         gain_sums_recv=dma((seq_devices,)),
     )
+    if gathered:
+        every = (seq_devices * rows, width)
+        ring_steps = seq_devices // 2
+        scratch.update(
+            gate_act_all=vmem(every, BF16), gate_slope_all=vmem(every, BF16),
+            skip_all=vmem((seq_devices, seqs, tokens, width), BF16),
+            inner_all=vmem((seq_devices, seqs, tokens, width), BF16),
+            xo_ring_sems=dma((2, ring_steps, 2)), xo_chan_sems=dma((seq_devices - 1, 6)),
+            skip_sems=dma((seqs, 2, ring_steps, 2)), inner_sems=dma((seqs, 2, ring_steps, 2)),
+            grad_small=vmem((small_rows, width), BF16), land_small=vmem((small_rows, width), BF16),
+            small_sems=dma((steps,)), result_sems=dma((5,)),
+        )
+    else:
+        late = (model + small_rows, width)
+        scratch.update(
+            cot=vmem((rows, model), BF16),
+            grad_w_out=vmem(w_out.shape, BF16), land_w_out=vmem(w_out.shape, BF16), w_out_sems=dma((steps,)),
+            grad_w_gate=vmem((model, width), BF16), land_w_gate=vmem((model, width), BF16),
+            w_gate_sems=dma((steps,)),
+            grad_w_inner=vmem(late, BF16), land_w_inner=vmem(late, BF16), full_w_inner=vmem(late, BF16),
+            w_inner_sems=dma((steps,)),
+        )
     names = list(operands) + list(outputs) + list(scratch)
     spaces = dict(lengths=pltpu.SMEM)
-    mixed_out, grad_inputs, gain, w_out_grad, w_gate_grad, late = pl.pallas_call(
+    mixed_out, grad_inputs, gain, w_in_grad, w_out_grad, small = pl.pallas_call(
         partial(layer_kernel, names, seq_devices),
         out_shape=tuple(jax.ShapeDtypeStruct(*item) for item in outputs.values()),
         in_specs=[pl.BlockSpec(memory_space=spaces.get(name, pltpu.VMEM)) for name in operands],
-        out_specs=tuple(pl.BlockSpec(memory_space=pltpu.VMEM) for _ in outputs),
+        out_specs=tuple(
+            pl.BlockSpec(memory_space=pl.ANY if gathered and name in ("out_w_in", "out_w_out") else pltpu.VMEM)
+            for name in outputs
+        ),
         scratch_shapes=list(scratch.values()),
         compiler_params=pltpu.CompilerParams(
             collective_id=0, has_side_effects=True, vmem_limit_bytes=VMEM_LIMIT
         ),
     )(*operands.values())
-    grad_w_out = jnp.concatenate([w_out_grad[:width], w_out_grad[width:]], axis=1).astype(F32)
-    grad_w_in = jnp.stack([late[:model], w_gate_grad]).astype(F32)
-    small = late[model:].astype(F32)
-    at = proj + low_rank + states
-    return (
-        mixed_out, grad_inputs, gain[0], grad_w_in, small[at : at + taps], small[at + taps],
-        small[:proj], small[proj : proj + low_rank], small[at + taps + 1],
-        small[proj + low_rank : at], small[at + taps + 2], grad_w_out,
-    )
+    parts = 4
+
+    def cut(shape, axis):
+        block = tuple(size // parts if k == axis else size for k, size in enumerate(shape))
+        return pl.BlockSpec(block, lambda i: tuple(i if k == axis else 0 for k in range(len(shape))))
+
+    def kept(shape):
+        return pl.BlockSpec(shape, lambda i: (0,) * len(shape))
+
+    def result(shape, spec, dtype=F32):
+        return jax.ShapeDtypeStruct(shape, dtype), spec
+
+    tokens_cut = cut(inputs.shape, 1)
+    w_in_cut, w_out_cut = (cut(w_in.shape, 1), cut(w_out.shape, 0))
+    wide_row = ((1, width), kept((1, width)))
+    results = [
+        result(inputs.shape, tokens_cut, BF16), result(inputs.shape, tokens_cut, BF16),
+        result((1, shard), kept((1, shard))), result(w_in.shape, w_in_cut),
+        result(conv_weight.shape, kept(conv_weight.shape)), result(*wide_row),
+        result(x_weight.shape, kept(x_weight.shape)), result(dt_weight.shape, kept(dt_weight.shape)),
+        result(*wide_row), result(log_decay.shape, kept(log_decay.shape)), result(*wide_row),
+        result(w_out.shape, w_out_cut),
+    ]
+    out = pl.pallas_call(
+        partial(finish_kernel, (proj, low_rank, states, taps)),
+        grid=(parts,),
+        out_shape=tuple(item[0] for item in results),
+        in_specs=[tokens_cut, tokens_cut, w_in_cut, w_out_cut, kept(small.shape), kept(gain.shape)],
+        out_specs=tuple(item[1] for item in results),
+        compiler_params=pltpu.CompilerParams(vmem_limit_bytes=VMEM_LIMIT),
+    )(mixed_out, grad_inputs, w_in_grad, w_out_grad, small, gain)
+    flat = (2, 5, 8, 10)
+    return tuple(value.reshape(-1) if k in flat else value for k, value in enumerate(out))
 
 
 def solution(mesh):

time: 179 us -> 129 us (0.72)
  Pallas kernels: 164 us -> 127 us
  local copies, waits for them, and re-layouts: 8.42 us -> 1.22 us
  other arithmetic: 4.96 us -> 0 us
    pallas_call x1, Pallas kernels: 164 us -> 121 us  [layer(): pl.pallas_call(partial(layer_kernel, names, seq_devices), out_shape=tuple...]
    pallas_call x0 -> x1, Pallas kernels: none -> 5.46 us  [layer(): pl.pallas_call(partial(finish_kernel, (proj, low_rank, states, taps)), gr...]
    convert_element_type x3 -> x0, other arithmetic: 4.96 us -> none  [the longest x1 2.29 us: layer(): grad_w_in = jnp.stack([late[:model], w_gate_grad]).astype(F32)]
    slice x7 -> x0, local copies, waits for them, and re-layouts: 4.58 us -> none  [the longest x1 1.35 us: layer(): gain[0]]
where the time goes in v2:
time: 129 us
  Pallas kernels  127 us (98%)
    pallas_call x1, Pallas kernels, layer(): pl.pallas_call(partial(layer_kernel, names, seq_devices), out_shape=tuple...  121 us
    pallas_call x1, Pallas kernels, layer(): pl.pallas_call(partial(finish_kernel, (proj, low_rank, states, taps)), gr...  5.46 us

profile of v2, /device:TPU:0, one launch (start us, length us, event | category | flops | bytes accessed | tf_op | source)
XLA Modules:
  0.0 129.0 jit_solution(17025676516036767565)
XLA Ops:
  0.6 1.2 reshape.48.refs_3_
  1.9 121.5 %shard_map.220 = (bf16[2,128,256]{2,1,0:T(8,128)(2,1)}, bf16[2,128,256]{2,1,0:T(8,128)(2,1)}, f32[8,256]{1,0:T(8,128)}, bf16[2,1024,512]{2,1,0:T(8,128)(2,1)}, b...) custom-call(bf16[2,128,256]{2,1,0:T(8,128)(2,1)} %refs_0_.1, s32[2]{0:T(128)} %refs_1_.1, ...), custom_call_target="tpu_custom_call" | custom-call | tf_op jit(solution)/shard_map/pallas_call | solution.py:1049
  123.4 5.5 %shard_map.221 = (bf16[2,128,256]{2,1,0:T(8,128)(2,1)}, bf16[2,128,256]{2,1,0:T(8,128)(2,1)}, f32[1,256]{1,0:T(1,128)}, f32[2,1024,512]{2,1,0:T(8,128)}, f32[4,5...) custom-call(bf16[2,128,256]{2,1,0:T(8,128)(2,1)} %get-tuple-element., ...), custom_call_target="tpu_custom_call" | custom-call | tf_op jit(solution)/shard_map/pallas_call | solution.py:1085

commit v3 on v2

--- a/solution.py
+++ b/solution.py
@@ -390,9 +390,57 @@
             copy.wait_send()
 
 
+class DirectSum:
+    def __init__(self, own, landing, full, sems, count, mine, chan):
+        self.own, self.landing, self.full, self.sems = (own, landing, full, sems)
+        self.count, self.mine, self.chan = (count, mine, chan)
+        self.rows = own.shape[0] // count
+        self.each(lambda k, peer: self.apart(peer, self.mine, peer).start())
+
+    def piece(self, ref, device):
+        return ref.at[pl.ds(pl.multiple_of(device * self.rows, self.rows), self.rows)]
+
+    def each(self, act):
+        def turn(k, _):
+            act(k, lax.rem(self.mine + k, self.count))
+            return 0
+
+        lax.fori_loop(1, self.count, turn, 0)
+
+    def apart(self, piece, source, peer):
+        return pltpu.make_async_remote_copy(
+            src_ref=self.piece(self.own, piece), dst_ref=self.landing.at[source],
+            send_sem=self.sems.at[0, peer], recv_sem=self.sems.at[1, source],
+            device_id=(peer, self.chan), device_id_type=MESH,
+        )
+
+    def back(self, source, peer):
+        return pltpu.make_async_remote_copy(
+            src_ref=self.piece(self.full, source), dst_ref=self.piece(self.full, source),
+            send_sem=self.sems.at[2, peer], recv_sem=self.sems.at[3, source],
+            device_id=(peer, self.chan), device_id_type=MESH,
+        )
+
+    def cross(self):
+        self.each(lambda k, peer: self.apart(peer, peer, peer).wait_recv())
+        mine = pl.ds(pl.multiple_of(self.mine * self.rows, self.rows), self.rows)
+
+        def add(k, total):
+            return total + self.landing[lax.rem(self.mine + k, self.count)].astype(F32)
+
+        total = lax.fori_loop(1, self.count, add, self.own[mine].astype(F32))
+        self.full[mine] = total.astype(BF16)
+        self.each(lambda k, peer: self.back(self.mine, peer).start())
+
+    def finish(self):
+        self.each(lambda k, peer: self.back(peer, peer).wait_recv())
+        self.each(lambda k, peer: self.apart(peer, self.mine, peer).wait_send())
+        self.each(lambda k, peer: self.back(self.mine, peer).wait_send())
+
+
 def layer_kernel(names, seq_devices, *refs):
     r = SimpleNamespace(**dict(zip(names, refs)))
-    x_ref, og_ref, win_ref, wout_ref = (r.inputs, r.out_grad, r.w_in, r.w_out)
+    x_ref, og_ref, win_ref, wout_ref = (r.inputs, r.out_grad, r.w_in_here, r.w_out_here)
     xw_ref, dtw_ref = (r.x_weight, r.dt_weight)
     seqs, tokens, shard = x_ref.shape
     model, width = win_ref.shape[1:]
@@ -407,6 +455,11 @@
     gathered = seq_devices <= MOST_GATHERED
     spot = me_s if gathered else 0
 
+    loads = []
+    for k, (src, dst) in enumerate(((r.w_in, r.w_in_here), (r.w_out, r.w_out_here))):
+        loads.append(pltpu.make_async_copy(src, dst, r.load_sems.at[k]))
+        loads[k].start()
+
     barrier = pltpu.get_barrier_semaphore()
 
     def greet(semaphore, device):
@@ -429,7 +482,7 @@
     gather_og = ChanGather(og_ref, lambda q: xo_ref.at[q, spot, 1], r.og_sems, me_c, core_peer, x_peer)
     xo_ref[me_c, spot, 0] = x_ref[...]
     xo_ref[me_c, spot, 1] = og_ref[...]
-    halo_ref[me_c, seqs] = jnp.broadcast_to(r.norm_gain[...], (HALO, shard))
+    halo_ref[me_c, seqs] = jnp.broadcast_to(r.norm_gain[...].astype(F32).reshape(1, shard), (HALO, shard)).astype(BF16)
     if gathered:
         gather_all = GridGather(
             lambda q, d: xo_ref.at[q, d], r.xo_ring_sems, r.xo_chan_sems, seq_devices, me_s, me_c, core_peer, x_peer
@@ -472,6 +525,8 @@
         squares = sum(jnp.sum(b * b, axis=1, keepdims=True) for b in blocks)
         root = lax.rsqrt(squares * (1.0 / model) + EPSILON)
         return root, [(b * root * gain_of(q)).astype(BF16) for q, b in enumerate(blocks)]
+
+    loads[0].wait()
 
     conv_sum = []
     normed_rows = []
@@ -509,6 +564,7 @@
         mine = pl.ds(s * tokens, tokens)
         r.gate_pre[mine, :] = dot(r.normed[normed_rows[s], :], win_ref[1])
     gather_og.finish()
+    loads[1].wait()
     for s in range(seqs):
         mine = pl.ds(s * tokens, tokens)
         cot = jnp.concatenate([xo_ref[q, spot, 1, s] for q in range(4)], axis=1)
@@ -593,7 +649,7 @@
         start_carried(ends_refs, s, me_s + 1, seq_devices)
     if gathered:
         gather_all.advance()
-        gather_all.relay(1)
+        gather_all.relay(2)
     for s in range(seqs):
         leaves = local_adjoints(r.decay, r.up, r.c, rate_ref, s * tokens, tokens)
         for k, lanes in enumerate(lane_chunks(width)):
@@ -665,6 +721,9 @@
                     partial(block_of, r.skip_all, s), r.skip_sems.at[s], seq_devices, me_s, me_c, s == 0
                 )
             )
+            if s == 0:
+                gather_all.advance()
+                gather_all.relay(2)
     out_part = dot(r.mixed[...], wout_ref[...])
     for q in range(4):
         r.out_blocks[q] = out_part[:, q * shard : (q + 1) * shard].astype(BF16)
@@ -675,18 +734,17 @@
     bits = [1 << k for k in range(seq_devices.bit_length() - 1)]
     turned = bits[1:] + bits[:1]
     if gathered:
-        gather_all.advance()
-        gather_all.relay(3)
+        skip_gathers[0].advance()
     else:
         r.grad_w_out[...] = dot(r.mixed[...], r.cot[...], ((0,), (0,))).astype(BF16)
         sums.append(SeqSum(r.grad_w_out, r.land_w_out, r.out_w_out, r.w_out_sems, bits, me_s, me_c))
         r.grad_w_gate[...] = dot(r.normed[...], r.grad_gate[...], ((0,), (0,))).astype(BF16)
         sums.append(SeqSum(r.grad_w_gate, r.land_w_gate, r.out_w_in.at[1], r.w_gate_sems, turned, me_s, me_c))
 
-    small = r.small
-    small[...] = jnp.zeros_like(small)
-    decay_row = proj + low_rank
-    tap_row = decay_row + states
+    early, later = (r.early, r.later)
+    early[...] = jnp.zeros_like(early)
+    later[...] = jnp.zeros_like(later)
+    skip_row = low_rank + states + 1
     low_sum, rim_copies, rate_sums = ([], [], [])
     has_right = (me_s < seq_devices - 1).astype(F32)
 
@@ -720,8 +778,8 @@
             )
         )
         r.grad_step_low[mine, :] = grad_step_low
-        small[tap_row + taps + 1, :] += jnp.sum(grad_step_pre, axis=0)
-        small[tap_row + taps + 2, :] += jnp.sum(r.up[mine, :] * act, axis=0)
+        early[skip_row - 1, :] += jnp.sum(grad_step_pre, axis=0)
+        early[skip_row, :] += jnp.sum(r.up[mine, :] * act, axis=0)
         r.grad_act[mine, :] = step * second + r.up[mine, :] * r.skip_gain[...]
 
     def through_conv(s):
@@ -737,10 +795,10 @@
         )
         grad_conv = grad_conv.astype(F32)
         r.grad_conv[s, :tokens, :] = grad_conv
-        small[tap_row + taps, :] += jnp.sum(grad_conv, axis=0)
+        later[proj + taps, :] += jnp.sum(grad_conv, axis=0)
         for k in range(taps):
             shifted = r.inner[s, HALO - taps + 1 + k : HALO - taps + 1 + k + tokens, :]
-            small[tap_row + k, :] += jnp.sum(grad_conv * shifted, axis=0)
+            later[proj + k, :] += jnp.sum(grad_conv * shifted, axis=0)
 
     def inner_of(s):
         mine = pl.ds(s * tokens, tokens)
@@ -762,46 +820,66 @@
             )
 
     def all_advance():
-        for item in sums + skip_gathers + inner_gathers:
+        for item in sums:
             item.advance()
 
-    def grid_advance(upto):
+    def skip_advance(s):
         if gathered:
-            gather_all.advance()
-            gather_all.relay(upto)
+            skip_gathers[s].advance()
+        else:
+            all_advance()
+
+    def inner_advance(s):
+        if gathered:
+            inner_gathers[s].advance()
+        else:
+            all_advance()
 
     def nothing():
         pass
 
-    scan_back(0, (scatter_out.cross, all_advance, partial(grid_advance, 5), all_advance))
+    scan_back(0, (nothing, scatter_out.cross, nothing, partial(skip_advance, 1)))
     after_scan(0)
-    scan_back(1, (low_sum[0].cross, all_advance, partial(through_conv, 0), all_advance))
+    skip_advance(0)
+    if gathered:
+        gather_all.advance()
+        gather_all.relay(4)
+    scan_back(1, (low_sum[0].cross, partial(skip_advance, 1), partial(through_conv, 0), nothing))
     after_scan(1)
+    skip_advance(0)
     inner_of(0)
+    for k, lanes in enumerate(lane_chunks(width)):
+        early[low_rank : low_rank + states, lanes] = (rate_sums[0][k] + rate_sums[1][k]) * rate_ref[:, lanes]
+    early[:low_rank, :] = dot(r.low[...], r.grad_step_low[...])
     low_sum[1].cross()
     if gathered:
+        r.early_own[...] = early[...].astype(BF16)
+        sum_early = DirectSum(
+            r.early_own, r.early_land, r.out_early, r.early_sems, seq_devices, me_s, me_c
+        )
         gather_all.relay(7)
         gather_all.finish()
         lax.fori_loop(1, 3, foreign, 0)
+    skip_advance(1)
     out_sum = scatter_out.finish()
     for s in range(seqs):
         r.mixed_out[s] = (x_ref[s].astype(F32) + out_sum[s * tokens : (s + 1) * tokens]).astype(BF16)
     through_conv(1)
-    for k, lanes in enumerate(lane_chunks(width)):
-        small[decay_row:tap_row, lanes] = (rate_sums[0][k] + rate_sums[1][k]) * rate_ref[:, lanes]
-    small[proj:decay_row, :] = dot(r.low[...], r.grad_step_low[...])
-    small[:proj, :] = dot(r.grad_proj[...], r.act[...].astype(BF16))
-    for item in sums:
-        item.advance()
+    later[:proj, :] = dot(r.grad_proj[...], r.act[...].astype(BF16))
+    if gathered:
+        r.later_own[...] = later[...].astype(BF16)
+        sum_later = DirectSum(
+            r.later_own, r.later_land, r.out_later, r.later_sems, seq_devices, me_s, me_c
+        )
     inner_of(1)
-
-    if gathered:
-        r.grad_small[...] = small[...].astype(BF16)
-        sums.append(SeqSum(r.grad_small, r.land_small, r.out_small, r.small_sems, bits, me_s, me_c))
-    else:
+    skip_advance(0)
+    inner_advance(0)
+
+    if not gathered:
         late = r.grad_w_inner
         late[:model, :] = dot(r.normed[...], r.grad_inner[...], ((0,), (0,))).astype(BF16)
-        late[model:, :] = small[...].astype(BF16)
+        late[model : model + early.shape[0], :] = early[...].astype(BF16)
+        late[model + early.shape[0] :, :] = later[...].astype(BF16)
         sums.append(SeqSum(late, r.land_w_inner, r.full_w_inner, r.w_inner_sems, bits, me_s, me_c))
     moment = None
     for q in range(4):
@@ -816,18 +894,19 @@
         r.gn_blocks, r.gn_first, r.gn_second, r.gn_sems, me_c, core_peer, x_peer,
         (r.moment, r.moment_first, r.moment_mid, r.moment_second),
     )
+    skip_advance(1)
+    if gathered:
+        sum_early.cross()
+    scatter_gn.cross()
+    inner_advance(1)
     if gathered:
         lax.fori_loop(3, 5, foreign, 0)
-    scatter_gn.cross()
-    all_advance()
-    if gathered:
-        lax.fori_loop(5, seq_devices, foreign, 0)
-        all_advance()
+    inner_advance(0)
     grad_normed, moment_row = scatter_gn.finish()
     moment = jnp.broadcast_to(moment_row[:1], (LANES, seqs * tokens)).T[:, :1]
     root = r.root[:, :1]
     values = x_ref[...].reshape(seqs * tokens, shard).astype(F32)
-    gains = r.norm_gain[...].astype(F32)
+    gains = gain_of(me_c)
     back = root * (grad_normed * gains) - values * (root * root * root) * moment * (1.0 / model)
     for s in range(seqs):
         mine = slice(s * tokens, (s + 1) * tokens)
@@ -850,9 +929,12 @@
 
     lax.fori_loop(1, seq_devices, start_gain, 0)
     if gathered:
-        all_advance()
+        inner_advance(1)
+        sum_later.cross()
+        lax.fori_loop(5, seq_devices, foreign, 0)
         for gather in skip_gathers:
             gather.finish()
+        inner_advance(0)
         count = seq_devices * seqs * tokens
 
         def mix(device, _):
@@ -878,11 +960,11 @@
             staged[rows, place : place + shard] = dot(r.gate_act_all[...], outs, ((0,), (0,))).astype(BF16)
             if place + shard == width:
                 deliver(staged.at[rows], r.out_w_out.at[:, pl.ds(half * width, width)])
-            all_advance()
+            if q % 2 == 1:
+                inner_advance(1 - q // 2)
         for q in range(4):
             rows = slice(q * shard, (q + 1) * shard)
             r.gate_act_all[rows, :] = dot(r.normed[:, rows], r.gate_slope_all[...], ((0,), (0,))).astype(BF16)
-            all_advance()
         deliver(r.gate_act_all.at[pl.ds(0, model)], r.out_w_in.at[1])
         for gather in inner_gathers:
             gather.finish()
@@ -896,7 +978,8 @@
                     r.gate_act_all.at[pl.ds(model + (q - 1) * shard, 2 * shard)],
                     r.out_w_in.at[0, pl.ds((q - 1) * shard, 2 * shard)],
                 )
-            all_advance()
+        sum_early.finish()
+        sum_later.finish()
     else:
         for step in range(max(item.total for item in sums)):
             all_advance()
@@ -921,14 +1004,15 @@
             copy.wait()
     else:
         r.out_w_in[0] = r.full_w_inner[:model, :]
-        r.out_small[...] = r.full_w_inner[model:, :]
+        r.out_early[...] = r.full_w_inner[model : model + early.shape[0], :]
+        r.out_later[...] = r.full_w_inner[model + early.shape[0] :, :]
     for s in range(seqs):
         wait_carried(ends_refs, s, me_s + 1, seq_devices)
         wait_carried(leaves_refs, s, 0, me_s)
 
 
 def finish_kernel(
-    rows_of, mixed_ref, inputs_ref, w_in_ref, w_out_ref, small_ref, gain_ref,
+    rows_of, mixed_ref, inputs_ref, w_in_ref, w_out_ref, early_ref, later_ref, gain_ref,
     mixed_out, grad_inputs, gain_out, w_in_out, conv_w_out, conv_b_out, x_out, dt_w_out, dt_b_out, decay_out,
     skip_out, w_out_out,
 ):
@@ -940,17 +1024,16 @@
     @pl.when(pl.program_id(0) == 0)
     def _():
         proj, low_rank, states, taps = rows_of
-        small = small_ref[...].astype(F32)
-        decay_row = proj + low_rank
-        tap_row = decay_row + states
+        early, later = (early_ref[...].astype(F32), later_ref[...].astype(F32))
+        skip_row = low_rank + states + 1
         gain_out[...] = gain_ref[0:1, :]
-        x_out[...] = small[:proj]
-        dt_w_out[...] = small[proj:decay_row]
-        decay_out[...] = small[decay_row:tap_row]
-        conv_w_out[...] = small[tap_row : tap_row + taps]
-        conv_b_out[...] = small[tap_row + taps : tap_row + taps + 1]
-        dt_b_out[...] = small[tap_row + taps + 1 : tap_row + taps + 2]
-        skip_out[...] = small[tap_row + taps + 2 : tap_row + taps + 3]
+        x_out[...] = later[:proj]
+        conv_w_out[...] = later[proj : proj + taps]
+        conv_b_out[...] = later[proj + taps : proj + taps + 1]
+        dt_w_out[...] = early[:low_rank]
+        decay_out[...] = early[low_rank : low_rank + states]
+        dt_b_out[...] = early[skip_row - 1 : skip_row]
+        skip_out[...] = early[skip_row : skip_row + 1]
 
 
 def layer(
@@ -962,27 +1045,29 @@
     _, model, width = w_in.shape
     states, low_rank, taps, proj = (log_decay.shape[0], dt_weight.shape[0], conv_weight.shape[0], x_weight.shape[0])
     rows = seqs * tokens
-    small_rows = proj + low_rank + states + taps + 3
-    grain = 16 * seq_devices
-    small_rows = -(-small_rows // grain) * grain
+    grain = 16 * seq_devices if seq_devices <= MOST_GATHERED else 8 * seq_devices
+    early_rows = -(-(low_rank + states + 2) // grain) * grain
+    later_rows = -(-(proj + taps + 1) // grain) * grain
     steps = 4 * (seq_devices.bit_length() - 1)
     gathered = seq_devices <= MOST_GATHERED
     dma = pltpu.SemaphoreType.DMA
     vmem = pltpu.VMEM
     operands = dict(
-        inputs=inputs, lengths=lengths, out_grad=out_grad, norm_gain=norm_gain.reshape(1, shard),
+        inputs=inputs, lengths=lengths, out_grad=out_grad, norm_gain=norm_gain,
         w_in=w_in, conv_weight=conv_weight, conv_bias=conv_bias.reshape(1, width),
         x_weight=x_weight, dt_weight=dt_weight, dt_bias=dt_bias.reshape(1, width),
         log_decay=log_decay, skip_gain=skip_gain.reshape(1, width), w_out=w_out,
     )
     outputs = dict(
         mixed_out=(inputs.shape, BF16), grad_inputs=(inputs.shape, BF16), grad_gain=((8, shard), F32),
-        out_w_in=(w_in.shape, BF16), out_w_out=(w_out.shape, BF16), out_small=((small_rows, width), BF16),
+        out_w_in=(w_in.shape, BF16), out_w_out=(w_out.shape, BF16),
+        out_early=((early_rows, width), BF16), out_later=((later_rows, width), BF16),
     )
     wide = (rows, width)
     scratch = dict(
         xo=vmem((4, seq_devices if gathered else 1, 2) + inputs.shape, BF16),
         halo=vmem((4, seqs + 1, HALO, shard), BF16), known=pltpu.SemaphoreType.REGULAR((8,)),
+        w_in_here=vmem(w_in.shape, BF16), w_out_here=vmem(w_out.shape, BF16), load_sems=dma((2,)),
         x_sems=dma((6,)), og_sems=dma((6,)), halo_sems=dma((8,)),
         rate=vmem((states, width), F32), rate2=vmem((states, width), F32),
         root=vmem((rows, LANES), F32), normed=vmem((seq_devices * rows if gathered else rows, model), BF16),
@@ -1018,7 +1103,7 @@
         gn_second=vmem((rows, shard), BF16), gn_sems=dma((10,)),
         moment=vmem((8, rows), F32), moment_first=vmem((8, rows), F32),
         moment_mid=vmem((8, rows), F32), moment_second=vmem((8, rows), F32),
-        small=vmem((small_rows, width), F32),
+        early=vmem((early_rows, width), F32), later=vmem((later_rows, width), F32),
         gain_sums=vmem((seq_devices, 8, shard), F32), gain_sums_send=dma((seq_devices,)),
         gain_sums_recv=dma((seq_devices,)),
     )
@@ -1031,11 +1116,13 @@
             inner_all=vmem((seq_devices, seqs, tokens, width), BF16),
             xo_ring_sems=dma((2, ring_steps, 2)), xo_chan_sems=dma((seq_devices - 1, 6)),
             skip_sems=dma((seqs, 2, ring_steps, 2)), inner_sems=dma((seqs, 2, ring_steps, 2)),
-            grad_small=vmem((small_rows, width), BF16), land_small=vmem((small_rows, width), BF16),
-            small_sems=dma((steps,)), result_sems=dma((5,)),
+            early_own=vmem((early_rows, width), BF16), later_own=vmem((later_rows, width), BF16),
+            early_land=vmem((seq_devices, early_rows // seq_devices, width), BF16),
+            later_land=vmem((seq_devices, later_rows // seq_devices, width), BF16),
+            early_sems=dma((4, seq_devices)), later_sems=dma((4, seq_devices)), result_sems=dma((5,)),
         )
     else:
-        late = (model + small_rows, width)
+        late = (model + early_rows + later_rows, width)
         scratch.update(
             cot=vmem((rows, model), BF16),
             grad_w_out=vmem(w_out.shape, BF16), land_w_out=vmem(w_out.shape, BF16), w_out_sems=dma((steps,)),
@@ -1045,8 +1132,8 @@
             w_inner_sems=dma((steps,)),
         )
     names = list(operands) + list(outputs) + list(scratch)
-    spaces = dict(lengths=pltpu.SMEM)
-    mixed_out, grad_inputs, gain, w_in_grad, w_out_grad, small = pl.pallas_call(
+    spaces = dict(lengths=pltpu.SMEM, w_in=pl.ANY, w_out=pl.ANY)
+    mixed_out, grad_inputs, gain, w_in_grad, w_out_grad, early, later = pl.pallas_call(
         partial(layer_kernel, names, seq_devices),
         out_shape=tuple(jax.ShapeDtypeStruct(*item) for item in outputs.values()),
         in_specs=[pl.BlockSpec(memory_space=spaces.get(name, pltpu.VMEM)) for name in operands],
@@ -1086,10 +1173,10 @@
         partial(finish_kernel, (proj, low_rank, states, taps)),
         grid=(parts,),
         out_shape=tuple(item[0] for item in results),
-        in_specs=[tokens_cut, tokens_cut, w_in_cut, w_out_cut, kept(small.shape), kept(gain.shape)],
+        in_specs=[tokens_cut, tokens_cut, w_in_cut, w_out_cut, kept(early.shape), kept(later.shape), kept(gain.shape)],
         out_specs=tuple(item[1] for item in results),
         compiler_params=pltpu.CompilerParams(vmem_limit_bytes=VMEM_LIMIT),
-    )(mixed_out, grad_inputs, w_in_grad, w_out_grad, small, gain)
+    )(mixed_out, grad_inputs, w_in_grad, w_out_grad, early, later, gain)
     flat = (2, 5, 8, 10)
     return tuple(value.reshape(-1) if k in flat else value for k, value in enumerate(out))
 

time: 129 us -> 117 us (0.907)
  Pallas kernels: 127 us -> 116 us
    pallas_call x1, Pallas kernels: 121 us -> 111 us  [layer(): pl.pallas_call(partial(layer_kernel, names, seq_devices), out_shape=tuple...]
where the time goes in v3:
time: 117 us
  Pallas kernels  116 us (99%)
    pallas_call x1, Pallas kernels, layer(): pl.pallas_call(partial(layer_kernel, names, seq_devices), out_shape=tuple...  111 us
    pallas_call x1, Pallas kernels, layer(): pl.pallas_call(partial(finish_kernel, (proj, low_rank, states, taps)), gr...  5.46 us

profile of v3, /device:TPU:0, one launch (start us, length us, event | category | flops | bytes accessed | tf_op | source)
XLA Modules:
  0.0 116.9 jit_solution(9190631746251980062)
XLA Ops:
  0.6 110.7 %shard_map.220 = (bf16[2,128,256]{2,1,0:T(8,128)(2,1)}, bf16[2,128,256]{2,1,0:T(8,128)(2,1)}, f32[8,256]{1,0:T(8,128)}, bf16[2,1024,512]{2,1,0:T(8,128)(2,1)}, b...) custom-call(bf16[2,128,256]{2,1,0:T(8,128)(2,1)} %refs_0_.1, s32[2]{0:T(128)} %refs_1_.1, ...), custom_call_target="tpu_custom_call" | custom-call | tf_op jit(solution)/shard_map/pallas_call | solution.py:1136
  111.3 5.5 %shard_map.221 = (bf16[2,128,256]{2,1,0:T(8,128)(2,1)}, bf16[2,128,256]{2,1,0:T(8,128)(2,1)}, f32[1,256]{1,0:T(1,128)}, f32[2,1024,512]{2,1,0:T(8,128)}, f32[4,5...) custom-call(bf16[2,128,256]{2,1,0:T(8,128)(2,1)} %get-tuple-element., ...), custom_call_target="tpu_custom_call" | custom-call | tf_op jit(solution)/shard_map/pallas_call | solution.py:1172

commit v4 on v3

--- a/solution.py
+++ b/solution.py
@@ -11,6 +11,24 @@
 EPSILON = 1e-05
 LANES = 128
 LOG2E = 1.4426950408889634
+ROWS, RELAY, SKIP, INNER, SMALL, OTHERS = range(6)
+SCHEDULE = {
+    1: ((ROWS, 0),),
+    3: ((ROWS, 0), (RELAY, 2),),
+    5: ((ROWS, 0),),
+    6: ((SKIP, 0),),
+    8: ((SKIP, 1),),
+    9: ((SKIP, 0),),
+    10: ((SKIP, 1),),
+    12: ((SKIP, 0), (ROWS, 0), (RELAY, 4),),
+    13: ((OTHERS, 1),),
+    14: ((SKIP, 1),),
+    16: ((INNER, 0),),
+    17: ((SKIP, 0), (INNER, 1),),
+    18: ((SKIP, 1), (RELAY, 6), (OTHERS, 2), (INNER, 0),),
+    19: ((INNER, 1), (RELAY, 7), (OTHERS, 3), (INNER, 0), (SMALL, 0), (OTHERS, 4), (INNER, 1),),
+    24: ((INNER, 0),),
+}
 VMEM_LIMIT = 60 * 2**20
 HALO = 16
 MOST_GATHERED = 8
@@ -280,9 +298,8 @@
             self.gathers[self.relayed].relay()
             self.relayed += 1
 
-    def finish(self):
-        self.ring.finish()
-        for gather in self.gathers:
+    def finish(self, step):
+        for gather in self.gathers[2 * step - 2 : 2 * step]:
             gather.finish()
 
 
@@ -438,6 +455,16 @@
         self.each(lambda k, peer: self.back(self.mine, peer).wait_send())
 
 
+def pack_small(early, later, low_rank, proj):
+    half = early.shape[1] // 2
+    rest = [early[low_rank:], later[proj:]]
+    spare = 2 * low_rank - proj - sum(part.shape[0] for part in rest)
+    rest.append(jnp.zeros((spare, early.shape[1]), early.dtype))
+    left = jnp.concatenate([later[:proj]] + rest, axis=0)
+    right = jnp.concatenate([early[:low_rank, :half], early[:low_rank, half:]], axis=0)
+    return jnp.concatenate([left, right], axis=1)
+
+
 def layer_kernel(names, seq_devices, *refs):
     r = SimpleNamespace(**dict(zip(names, refs)))
     x_ref, og_ref, win_ref, wout_ref = (r.inputs, r.out_grad, r.w_in_here, r.w_out_here)
@@ -472,7 +499,12 @@
     pl.semaphore_wait(barrier, len(first_peers))
 
     xo_ref, halo_ref = (r.xo, r.halo)
-    gather_x = ChanGather(x_ref, lambda q: xo_ref.at[q, spot, 0], r.x_sems, me_c, core_peer, x_peer)
+    gather_x = [
+        ChanGather(
+            x_ref.at[s], partial(lambda s, q: xo_ref.at[q, spot, 0, s], s), r.x_sems.at[s], me_c, core_peer, x_peer
+        )
+        for s in range(seqs)
+    ]
     halo_copy = send(
         x_ref.at[:, pl.ds(tokens - HALO, HALO), :], halo_ref.at[me_c, pl.ds(0, seqs)],
         r.halo_sems.at[6], r.halo_sems.at[7], (right, me_c),
@@ -487,16 +519,38 @@
         gather_all = GridGather(
             lambda q, d: xo_ref.at[q, d], r.xo_ring_sems, r.xo_chan_sems, seq_devices, me_s, me_c, core_peer, x_peer
         )
+    skip_gathers, inner_gathers, small_sums, sums = ([], [], [], [])
+
+    def hook(place):
+        if not gathered:
+            if place > 6:
+                for item in sums:
+                    item.advance()
+            return
+        for kind, which in SCHEDULE.get(place, ()):
+            if kind == ROWS:
+                gather_all.advance()
+            elif kind == RELAY:
+                gather_all.relay(which)
+            elif kind == SKIP:
+                skip_gathers[which].advance()
+            elif kind == INNER:
+                inner_gathers[which].advance()
+            elif kind == SMALL:
+                small_sums[0].cross()
+            else:
+                foreign_pair(which)
+
     halo_copy.wait_recv()
     gather_halo = ChanGather(
         halo_ref.at[me_c], lambda q: halo_ref.at[q], r.halo_sems, me_c, core_peer, x_peer
     )
-    gather_x.relay()
+    for s in range(seqs):
+        gather_x[s].relay()
     gather_halo.relay()
-    gather_x.finish()
+    gather_x[0].finish()
     gather_halo.finish()
     halo_copy.wait_send()
-    gather_og.relay()
 
     reaches = [1]
     while 2 * reaches[-1] < seq_devices // 2:
@@ -508,8 +562,6 @@
             for step in (reaches[k + 1], -reaches[k + 1]):
                 greet(r.known.at[k + 1], (ring_device(position + step, seq_devices), me_c))
 
-    hear(0)
-
     rate_ref, rate2_ref = (r.rate, r.rate2)
     rate_ref[...] = -jnp.exp(r.log_decay[...])
     rate2_ref[...] = rate_ref[...] * LOG2E
@@ -526,6 +578,7 @@
         root = lax.rsqrt(squares * (1.0 / model) + EPSILON)
         return root, [(b * root * gain_of(q)).astype(BF16) for q, b in enumerate(blocks)]
 
+    hear(0)
     loads[0].wait()
 
     conv_sum = []
@@ -533,6 +586,8 @@
     has_left = (me_s > 0).astype(F32)
     for s in range(seqs):
         mine = pl.ds(s * tokens, tokens)
+        if s > 0:
+            gather_x[s].finish()
         root, rows = normalize([xo_ref[q, spot, 0, s].astype(F32) for q in range(4)])
         _, before = normalize([halo_ref[q, s].astype(F32) for q in range(4)])
         r.root[mine, :] = jnp.broadcast_to(root, (tokens, LANES))
@@ -558,8 +613,10 @@
                 r.proj_sems.at[s], core_peer, x_peer,
             )
         )
+    gather_og.relay()
     for s in range(seqs):
         conv_sum[s].cross()
+    hook(0)
     for s in range(seqs):
         mine = pl.ds(s * tokens, tokens)
         r.gate_pre[mine, :] = dot(r.normed[normed_rows[s], :], win_ref[1])
@@ -579,8 +636,7 @@
             r.gate_slope_all[rows, :] = (grad_mixed * silu_slope(gate, sigmoid)).astype(BF16)
         else:
             r.cot[mine, :] = (cot.astype(F32) * mask_of(s, tokens, 0)).astype(BF16)
-    if gathered:
-        gather_all.advance()
+    hook(1)
 
     totals_ref = r.totals
     step_totals = []
@@ -596,6 +652,7 @@
         r.drive[mine, :] = step * r.act[mine, :]
         step_totals.append(jnp.sum(step, axis=0, keepdims=True))
         spread_maps(projected[low_rank:], r.b, r.c, s * tokens, tokens)
+    hook(2)
     totals_ref[me_s] = jnp.concatenate(step_totals + [jnp.zeros((8 - seqs, width), F32)], axis=0)
 
     def seq_device(k):
@@ -647,14 +704,14 @@
         for k, lanes in enumerate(lane_chunks(width)):
             r.ends[s, me_s, :, lanes] = ends[k].astype(BF16)
         start_carried(ends_refs, s, me_s + 1, seq_devices)
-    if gathered:
-        gather_all.advance()
-        gather_all.relay(2)
+    hook(3)
     for s in range(seqs):
         leaves = local_adjoints(r.decay, r.up, r.c, rate_ref, s * tokens, tokens)
         for k, lanes in enumerate(lane_chunks(width)):
             r.leaves[s, me_s, :, lanes] = leaves[k].astype(BF16)
         start_carried(leaves_refs, s, 0, me_s)
+
+    hook(4)
 
     def wait_totals(k, _):
         peer = lax.rem(me_s + k, seq_devices)
@@ -682,13 +739,16 @@
 
         return lax.fori_loop(0, count, turn, jnp.zeros((states, width), F32))
 
-    skip_gathers, inner_gathers = ([], [])
-
     def block_of(ref, s, device):
         return ref.at[device, s]
 
-    def foreign(k, _):
-        device = lax.rem(me_s + k, seq_devices)
+    def foreign_pair(step):
+        gather_all.finish(step)
+        last = 2 * step == seq_devices
+        lax.fori_loop(0, 1 if last else 2, partial(foreign, step), 0)
+
+    def foreign(step, side, _):
+        device = ring_device(position + step - 2 * step * side, seq_devices)
         rows = pl.ds(pl.multiple_of(device * (seqs * tokens), seqs * tokens), seqs * tokens)
         blocks = [xo_ref[q, device, 0].reshape(seqs * tokens, shard).astype(F32) for q in range(4)]
         normed = jnp.concatenate(normalize(blocks)[1], axis=1)
@@ -721,21 +781,18 @@
                     partial(block_of, r.skip_all, s), r.skip_sems.at[s], seq_devices, me_s, me_c, s == 0
                 )
             )
-            if s == 0:
-                gather_all.advance()
-                gather_all.relay(2)
+        if s == 0:
+            hook(5)
     out_part = dot(r.mixed[...], wout_ref[...])
     for q in range(4):
         r.out_blocks[q] = out_part[:, q * shard : (q + 1) * shard].astype(BF16)
     scatter_out = ChanScatter(
         r.out_blocks, r.out_first, r.out_second, r.out_sems, me_c, core_peer, x_peer
     )
-    sums = []
     bits = [1 << k for k in range(seq_devices.bit_length() - 1)]
     turned = bits[1:] + bits[:1]
-    if gathered:
-        skip_gathers[0].advance()
-    else:
+    hook(6)
+    if not gathered:
         r.grad_w_out[...] = dot(r.mixed[...], r.cot[...], ((0,), (0,))).astype(BF16)
         sums.append(SeqSum(r.grad_w_out, r.land_w_out, r.out_w_out, r.w_out_sems, bits, me_s, me_c))
         r.grad_w_gate[...] = dot(r.normed[...], r.grad_gate[...], ((0,), (0,))).astype(BF16)
@@ -819,61 +876,41 @@
                 )
             )
 
-    def all_advance():
-        for item in sums:
-            item.advance()
-
-    def skip_advance(s):
-        if gathered:
-            skip_gathers[s].advance()
-        else:
-            all_advance()
-
-    def inner_advance(s):
-        if gathered:
-            inner_gathers[s].advance()
-        else:
-            all_advance()
-
     def nothing():
         pass
 
-    scan_back(0, (nothing, scatter_out.cross, nothing, partial(skip_advance, 1)))
+    def scatter_and_hook():
+        scatter_out.cross()
+        hook(7)
+
+    scan_back(0, (nothing, scatter_and_hook, nothing, partial(hook, 8)))
     after_scan(0)
-    skip_advance(0)
-    if gathered:
-        gather_all.advance()
-        gather_all.relay(4)
-    scan_back(1, (low_sum[0].cross, partial(skip_advance, 1), partial(through_conv, 0), nothing))
+    hook(9)
+    scan_back(1, (low_sum[0].cross, partial(hook, 10), partial(through_conv, 0), partial(hook, 11)))
     after_scan(1)
-    skip_advance(0)
+    hook(12)
     inner_of(0)
     for k, lanes in enumerate(lane_chunks(width)):
         early[low_rank : low_rank + states, lanes] = (rate_sums[0][k] + rate_sums[1][k]) * rate_ref[:, lanes]
     early[:low_rank, :] = dot(r.low[...], r.grad_step_low[...])
     low_sum[1].cross()
-    if gathered:
-        r.early_own[...] = early[...].astype(BF16)
-        sum_early = DirectSum(
-            r.early_own, r.early_land, r.out_early, r.early_sems, seq_devices, me_s, me_c
-        )
-        gather_all.relay(7)
-        gather_all.finish()
-        lax.fori_loop(1, 3, foreign, 0)
-    skip_advance(1)
+    hook(13)
     out_sum = scatter_out.finish()
     for s in range(seqs):
         r.mixed_out[s] = (x_ref[s].astype(F32) + out_sum[s * tokens : (s + 1) * tokens]).astype(BF16)
+    hook(14)
     through_conv(1)
     later[:proj, :] = dot(r.grad_proj[...], r.act[...].astype(BF16))
     if gathered:
-        r.later_own[...] = later[...].astype(BF16)
-        sum_later = DirectSum(
-            r.later_own, r.later_land, r.out_later, r.later_sems, seq_devices, me_s, me_c
-        )
+        r.small_own[...] = pack_small(
+            early[: skip_row + 1, :], later[: proj + taps + 1, :], low_rank, proj
+        ).astype(BF16)
+        small_sums.append(
+            DirectSum(r.small_own, r.small_land, r.out_small, r.small_sems, seq_devices, me_s, me_c)
+        )
+    hook(15)
     inner_of(1)
-    skip_advance(0)
-    inner_advance(0)
+    hook(16)
 
     if not gathered:
         late = r.grad_w_inner
@@ -894,14 +931,9 @@
         r.gn_blocks, r.gn_first, r.gn_second, r.gn_sems, me_c, core_peer, x_peer,
         (r.moment, r.moment_first, r.moment_mid, r.moment_second),
     )
-    skip_advance(1)
-    if gathered:
-        sum_early.cross()
+    hook(17)
     scatter_gn.cross()
-    inner_advance(1)
-    if gathered:
-        lax.fori_loop(3, 5, foreign, 0)
-    inner_advance(0)
+    hook(18)
     grad_normed, moment_row = scatter_gn.finish()
     moment = jnp.broadcast_to(moment_row[:1], (LANES, seqs * tokens)).T[:, :1]
     root = r.root[:, :1]
@@ -928,13 +960,11 @@
         return 0
 
     lax.fori_loop(1, seq_devices, start_gain, 0)
+    hook(19)
     if gathered:
-        inner_advance(1)
-        sum_later.cross()
-        lax.fori_loop(5, seq_devices, foreign, 0)
+        gather_all.ring.finish()
         for gather in skip_gathers:
             gather.finish()
-        inner_advance(0)
         count = seq_devices * seqs * tokens
 
         def mix(device, _):
@@ -945,6 +975,7 @@
             return 0
 
         lax.fori_loop(0, seq_devices, mix, 0)
+        hook(20)
         results = []
 
         def deliver(src, dst):
@@ -960,11 +991,11 @@
             staged[rows, place : place + shard] = dot(r.gate_act_all[...], outs, ((0,), (0,))).astype(BF16)
             if place + shard == width:
                 deliver(staged.at[rows], r.out_w_out.at[:, pl.ds(half * width, width)])
-            if q % 2 == 1:
-                inner_advance(1 - q // 2)
+            hook(21 + q)
         for q in range(4):
             rows = slice(q * shard, (q + 1) * shard)
             r.gate_act_all[rows, :] = dot(r.normed[:, rows], r.gate_slope_all[...], ((0,), (0,))).astype(BF16)
+            hook(25 + q)
         deliver(r.gate_act_all.at[pl.ds(0, model)], r.out_w_in.at[1])
         for gather in inner_gathers:
             gather.finish()
@@ -978,11 +1009,11 @@
                     r.gate_act_all.at[pl.ds(model + (q - 1) * shard, 2 * shard)],
                     r.out_w_in.at[0, pl.ds((q - 1) * shard, 2 * shard)],
                 )
-        sum_early.finish()
-        sum_later.finish()
+        small_sums[0].finish()
     else:
         for step in range(max(item.total for item in sums)):
-            all_advance()
+            for item in sums:
+                item.advance()
 
     def take_gain(k, _):
         peer = lax.rem(me_s + k, seq_devices)
@@ -1004,15 +1035,18 @@
             copy.wait()
     else:
         r.out_w_in[0] = r.full_w_inner[:model, :]
-        r.out_early[...] = r.full_w_inner[model : model + early.shape[0], :]
-        r.out_later[...] = r.full_w_inner[model + early.shape[0] :, :]
+        full, rest = (r.full_w_inner, model + early.shape[0])
+        r.out_small[...] = pack_small(
+            full[model : model + skip_row + 1, :].astype(F32), full[rest : rest + proj + taps + 1, :].astype(F32),
+            low_rank, proj,
+        ).astype(BF16)
     for s in range(seqs):
         wait_carried(ends_refs, s, me_s + 1, seq_devices)
         wait_carried(leaves_refs, s, 0, me_s)
 
 
 def finish_kernel(
-    rows_of, mixed_ref, inputs_ref, w_in_ref, w_out_ref, early_ref, later_ref, gain_ref,
+    rows_of, mixed_ref, inputs_ref, w_in_ref, w_out_ref, small_ref, gain_ref,
     mixed_out, grad_inputs, gain_out, w_in_out, conv_w_out, conv_b_out, x_out, dt_w_out, dt_b_out, decay_out,
     skip_out, w_out_out,
 ):
@@ -1024,16 +1058,18 @@
     @pl.when(pl.program_id(0) == 0)
     def _():
         proj, low_rank, states, taps = rows_of
-        early, later = (early_ref[...].astype(F32), later_ref[...].astype(F32))
-        skip_row = low_rank + states + 1
+        small, width = (small_ref[...].astype(F32), x_out.shape[1])
+        left, right = (small[:, :width], small[:, width:])
+        tap_row = proj + states + 2
         gain_out[...] = gain_ref[0:1, :]
-        x_out[...] = later[:proj]
-        conv_w_out[...] = later[proj : proj + taps]
-        conv_b_out[...] = later[proj + taps : proj + taps + 1]
-        dt_w_out[...] = early[:low_rank]
-        decay_out[...] = early[low_rank : low_rank + states]
-        dt_b_out[...] = early[skip_row - 1 : skip_row]
-        skip_out[...] = early[skip_row : skip_row + 1]
+        x_out[...] = left[:proj]
+        dt_w_out[:, : width // 2] = right[:low_rank]
+        dt_w_out[:, width // 2 :] = right[low_rank:]
+        decay_out[...] = left[proj : proj + states]
+        dt_b_out[...] = left[tap_row - 2 : tap_row - 1]
+        skip_out[...] = left[tap_row - 1 : tap_row]
+        conv_w_out[...] = left[tap_row : tap_row + taps]
+        conv_b_out[...] = left[tap_row + taps : tap_row + taps + 1]
 
 
 def layer(
@@ -1061,14 +1097,14 @@
     outputs = dict(
         mixed_out=(inputs.shape, BF16), grad_inputs=(inputs.shape, BF16), grad_gain=((8, shard), F32),
         out_w_in=(w_in.shape, BF16), out_w_out=(w_out.shape, BF16),
-        out_early=((early_rows, width), BF16), out_later=((later_rows, width), BF16),
+        out_small=((2 * low_rank, width + width // 2), BF16),
     )
     wide = (rows, width)
     scratch = dict(
         xo=vmem((4, seq_devices if gathered else 1, 2) + inputs.shape, BF16),
         halo=vmem((4, seqs + 1, HALO, shard), BF16), known=pltpu.SemaphoreType.REGULAR((8,)),
         w_in_here=vmem(w_in.shape, BF16), w_out_here=vmem(w_out.shape, BF16), load_sems=dma((2,)),
-        x_sems=dma((6,)), og_sems=dma((6,)), halo_sems=dma((8,)),
+        x_sems=dma((seqs, 6)), og_sems=dma((6,)), halo_sems=dma((8,)),
         rate=vmem((states, width), F32), rate2=vmem((states, width), F32),
         root=vmem((rows, LANES), F32), normed=vmem((seq_devices * rows if gathered else rows, model), BF16),
         inner=vmem((seqs, HALO + tokens, width), F32),
@@ -1116,10 +1152,9 @@
             inner_all=vmem((seq_devices, seqs, tokens, width), BF16),
             xo_ring_sems=dma((2, ring_steps, 2)), xo_chan_sems=dma((seq_devices - 1, 6)),
             skip_sems=dma((seqs, 2, ring_steps, 2)), inner_sems=dma((seqs, 2, ring_steps, 2)),
-            early_own=vmem((early_rows, width), BF16), later_own=vmem((later_rows, width), BF16),
-            early_land=vmem((seq_devices, early_rows // seq_devices, width), BF16),
-            later_land=vmem((seq_devices, later_rows // seq_devices, width), BF16),
-            early_sems=dma((4, seq_devices)), later_sems=dma((4, seq_devices)), result_sems=dma((5,)),
+            small_own=vmem((2 * low_rank, width + width // 2), BF16),
+            small_land=vmem((seq_devices, 2 * low_rank // seq_devices, width + width // 2), BF16),
+            small_sems=dma((4, seq_devices)), result_sems=dma((5,)),
         )
     else:
         late = (model + early_rows + later_rows, width)
@@ -1133,7 +1168,7 @@
         )
     names = list(operands) + list(outputs) + list(scratch)
     spaces = dict(lengths=pltpu.SMEM, w_in=pl.ANY, w_out=pl.ANY)
-    mixed_out, grad_inputs, gain, w_in_grad, w_out_grad, early, later = pl.pallas_call(
+    mixed_out, grad_inputs, gain, w_in_grad, w_out_grad, small = pl.pallas_call(
         partial(layer_kernel, names, seq_devices),
         out_shape=tuple(jax.ShapeDtypeStruct(*item) for item in outputs.values()),
         in_specs=[pl.BlockSpec(memory_space=spaces.get(name, pltpu.VMEM)) for name in operands],
@@ -1173,10 +1208,10 @@
         partial(finish_kernel, (proj, low_rank, states, taps)),
         grid=(parts,),
         out_shape=tuple(item[0] for item in results),
-        in_specs=[tokens_cut, tokens_cut, w_in_cut, w_out_cut, kept(early.shape), kept(later.shape), kept(gain.shape)],
+        in_specs=[tokens_cut, tokens_cut, w_in_cut, w_out_cut, kept(small.shape), kept(gain.shape)],
         out_specs=tuple(item[1] for item in results),
         compiler_params=pltpu.CompilerParams(vmem_limit_bytes=VMEM_LIMIT),
-    )(mixed_out, grad_inputs, w_in_grad, w_out_grad, early, later, gain)
+    )(mixed_out, grad_inputs, w_in_grad, w_out_grad, small, gain)
     flat = (2, 5, 8, 10)
     return tuple(value.reshape(-1) if k in flat else value for k, value in enumerate(out))
 

time: 117 us -> 113 us (0.966)
  Pallas kernels: 116 us -> 112 us
    pallas_call x1, Pallas kernels: 111 us -> 106 us  [layer(): pl.pallas_call(partial(layer_kernel, names, seq_devices), out_shape=tuple...]
where the time goes in v4:
time: 113 us; the launch traced here: 112 us
  Pallas kernels  112 us (99%)
    pallas_call x1, Pallas kernels, layer(): pl.pallas_call(partial(layer_kernel, names, seq_devices), out_shape=tuple...  106 us
    pallas_call x1, Pallas kernels, layer(): pl.pallas_call(partial(finish_kernel, (proj, low_rank, states, taps)), gr...  5.44 us

profile of v4, /device:TPU:0, one launch (start us, length us, event | category | flops | bytes accessed | tf_op | source)
XLA Modules:
  0.0 112.4 jit_solution(18442650285850772119)
XLA Ops:
  0.6 106.2 %shard_map.220 = (bf16[2,128,256]{2,1,0:T(8,128)(2,1)}, bf16[2,128,256]{2,1,0:T(8,128)(2,1)}, f32[8,256]{1,0:T(8,128)}, bf16[2,1024,512]{2,1,0:T(8,128)(2,1)}, b...) custom-call(bf16[2,128,256]{2,1,0:T(8,128)(2,1)} %refs_0_.1, s32[2]{0:T(128)} %refs_1_.1, ...), custom_call_target="tpu_custom_call" | custom-call | tf_op jit(solution)/shard_map/pallas_call | solution.py:1171
  106.8 5.4 %shard_map.221 = (bf16[2,128,256]{2,1,0:T(8,128)(2,1)}, bf16[2,128,256]{2,1,0:T(8,128)(2,1)}, f32[1,256]{1,0:T(1,128)}, f32[2,1024,512]{2,1,0:T(8,128)}, f32[4,5...) custom-call(bf16[2,128,256]{2,1,0:T(8,128)(2,1)} %get-tuple-element., ...), custom_call_target="tpu_custom_call" | custom-call | tf_op jit(solution)/shard_map/pallas_call | solution.py:1207

commit v5 on v4

--- a/solution.py
+++ b/solution.py
@@ -311,14 +311,14 @@
 
     def cross(self):
         self.copies[0].wait_recv()
-        self.middle[...] = self.own[...] + self.first[...]
+        self.middle[...] = (self.own[...].astype(F32) + self.first[...].astype(F32)).astype(BF16)
         self.copies.append(send(self.middle, self.second, self.sems.at[2], self.sems.at[3], self.x_peer))
 
     def finish(self):
         self.copies[1].wait_recv()
         for copy in self.copies:
             copy.wait_send()
-        return self.middle[...] + self.second[...]
+        return self.middle[...].astype(F32) + self.second[...].astype(F32)
 
 
 class ChanScatter:
@@ -606,7 +606,7 @@
         r.conv_pre[mine, :] = conv_pre
         act = (conv_pre * jax.nn.sigmoid(conv_pre)).astype(BF16)
         r.act[mine, :] = act.astype(F32)
-        r.proj_own[s] = dot(xw_ref[...], act, ((1,), (1,)))
+        r.proj_own[s] = dot(xw_ref[...], act, ((1,), (1,))).astype(BF16)
         conv_sum.append(
             ChanSum(
                 r.proj_own.at[s], r.proj_first.at[s], r.proj_second.at[s], r.proj_mid.at[s],
@@ -825,9 +825,9 @@
         grad_step_pre = (r.first_sum[...] + act * second) * jax.nn.sigmoid(step_pre)
         grad_step_low = grad_step_pre.astype(BF16)
         own = r.proj_own.at[s]
-        own[:low_rank, :] = dot(dtw_ref[...], grad_step_low, ((1,), (1,)))
-        own[low_rank : low_rank + states, :] = map_sums(r.adjoint, r.drive[mine, :], states, 0, tokens)
-        own[low_rank + states :, :] = map_sums(r.state, r.up[mine, :], states, s * tokens, tokens)
+        own[:low_rank, :] = dot(dtw_ref[...], grad_step_low, ((1,), (1,))).astype(BF16)
+        own[low_rank : low_rank + states, :] = map_sums(r.adjoint, r.drive[mine, :], states, 0, tokens).astype(BF16)
+        own[low_rank + states :, :] = map_sums(r.state, r.up[mine, :], states, s * tokens, tokens).astype(BF16)
         low_sum.append(
             ChanSum(
                 own, r.back_first.at[s], r.back_second.at[s], r.back_mid.at[s],
@@ -1110,11 +1110,11 @@
         inner=vmem((seqs, HALO + tokens, width), F32),
         conv_pre=vmem(wide, F32), act=vmem(wide, F32), gate_pre=vmem(wide, F32),
         grad_mixed=vmem(wide, F32), up=vmem(wide, F32),
-        proj_own=vmem((seqs, proj, tokens), F32), proj_first=vmem((seqs, proj, tokens), F32),
-        proj_second=vmem((seqs, proj, tokens), F32), proj_mid=vmem((seqs, proj, tokens), F32),
+        proj_own=vmem((seqs, proj, tokens), BF16), proj_first=vmem((seqs, proj, tokens), BF16),
+        proj_second=vmem((seqs, proj, tokens), BF16), proj_mid=vmem((seqs, proj, tokens), BF16),
         proj_sems=dma((seqs, 4)),
-        back_first=vmem((seqs, proj, tokens), F32), back_second=vmem((seqs, proj, tokens), F32),
-        back_mid=vmem((seqs, proj, tokens), F32), back_sems=dma((seqs, 4)),
+        back_first=vmem((seqs, proj, tokens), BF16), back_second=vmem((seqs, proj, tokens), BF16),
+        back_mid=vmem((seqs, proj, tokens), BF16), back_sems=dma((seqs, 4)),
         low=vmem((low_rank, rows), BF16), step_pre=vmem(wide, F32), step=vmem(wide, F32),
         drive=vmem(wide, F32), b=vmem((rows, states, LANES), F32), c=vmem((rows, states, LANES), F32),
         decay=vmem((rows, states, width), F32),
@@ -1181,7 +1181,7 @@
             collective_id=0, has_side_effects=True, vmem_limit_bytes=VMEM_LIMIT
         ),
     )(*operands.values())
-    parts = 4
+    parts = 2
 
     def cut(shape, axis):
         block = tuple(size // parts if k == axis else size for k, size in enumerate(shape))

time: 113 us -> 111 us (0.982)
  Pallas kernels: 112 us -> 110 us
where the time goes in v5:
time: 111 us
  Pallas kernels  110 us (99%)
    pallas_call x1, Pallas kernels, layer(): pl.pallas_call(partial(layer_kernel, names, seq_devices), out_shape=tuple...  105 us
    pallas_call x1, Pallas kernels, layer(): pl.pallas_call(partial(finish_kernel, (proj, low_rank, states, taps)), gr...  4.67 us

profile of v5, /device:TPU:0, one launch (start us, length us, event | category | flops | bytes accessed | tf_op | source)
XLA Modules:
  0.0 110.8 jit_solution(10683755203711534556)
XLA Ops:
  0.6 105.3 %shard_map.220 = (bf16[2,128,256]{2,1,0:T(8,128)(2,1)}, bf16[2,128,256]{2,1,0:T(8,128)(2,1)}, f32[8,256]{1,0:T(8,128)}, bf16[2,1024,512]{2,1,0:T(8,128)(2,1)}, b...) custom-call(bf16[2,128,256]{2,1,0:T(8,128)(2,1)} %refs_0_.1, s32[2]{0:T(128)} %refs_1_.1, ...), custom_call_target="tpu_custom_call" | custom-call | tf_op jit(solution)/shard_map/pallas_call | solution.py:1171
  105.9 4.7 %shard_map.221 = (bf16[2,128,256]{2,1,0:T(8,128)(2,1)}, bf16[2,128,256]{2,1,0:T(8,128)(2,1)}, f32[1,256]{1,0:T(1,128)}, f32[2,1024,512]{2,1,0:T(8,128)}, f32[4,5...) custom-call(bf16[2,128,256]{2,1,0:T(8,128)(2,1)} %get-tuple-element., ...), custom_call_target="tpu_custom_call" | custom-call | tf_op jit(solution)/shard_map/pallas_call | solution.py:1207
